TPU v7x, 32 devices: a whole 2x2x4 slice. The times are simulated.
32 devices in a mesh: rows: 16 (over z, y, x), mp: 2 (over core).
Axes of the slice: x: 2, y: 2, z: 4, core: 2. Of those that a mesh axis runs over, the one named last changes fastest.
Arguments:
- params: float32 [329728], P(('rows', 'mp'))
- momentum: float32 [329728], P(('rows', 'mp')), may hold values from -0.0008544922 to 0.0008544922
- average: float32 [329728], P(('rows', 'mp'))
- table: float32 [1024, 256], P('rows'), may hold values from -5 to 5
- code_first: float32 [1024, 256], P('rows'), may hold values from -5.340576e-05 to 5.340576e-05
- code_second: float32 [1024, 256], P('rows'), may hold values from 9.765625e-13 to 3.90625e-12
- coords: float32 [3, 131072], P(None, ('rows', 'mp')), may hold values from -3 to 3
- targets: float32 [131072], P(('rows', 'mp')), may hold values from -0.6 to 0.6
- segment_ids: int32 [131072], P(('rows', 'mp')), may hold values from -1 to 63, as said below
- shape_code: int32 [64], replicated, may hold values from 0 to 1023, as said below
Outputs:
- loss: float32 [], replicated
- new_momentum: float32 [329728], P(('rows', 'mp'))
- new_params: float32 [329728], P(('rows', 'mp'))
- new_average: float32 [329728], P(('rows', 'mp'))
- new_table: float32 [1024, 256], P('rows')
- new_first: float32 [1024, 256], P('rows')
- new_second: float32 [1024, 256], P('rows')
Inputs may be any that keep to these rules, and one draw needn't show every extreme that they name: `segment_ids`: devices counted over rows+mp in mesh order, each holding 4096 consecutive samples: the first 256 samples of every device belong to one shape, the same on all devices, and are never padding; the other samples of device d are -1 or belong to shapes d * 2 to d * 2 + 1 in non-decreasing order, each of these shapes with at least one sample there. `shape_code`: distinct table rows.
All inputs are finite; a program needn't handle non-finite values.
Results may differ from a plain program's by a relative error of at most 0.0003.
Values sent between devices are 32-bit elements; how exact they have to be, the bound alone decides.
A program may use at most 64 MiB of HBM per device.

v0:
```python
import jax
import jax.numpy as jnp
from jax import lax
from jax.sharding import PartitionSpec as P

CODE = 256
H2 = 512
SHAPES_DEV = 2
STEP = 10


PRECISE = lax.Precision.HIGHEST
CLAMP_DELTA = 0.1
SMOOTH = 0.01
PRIOR_WEIGHT = 0.001
LEARN_RATE = 200.0
MOMENTUM_DECAY = 0.9
AVERAGE_DECAY = 0.9
CODE_RATE = 0.5
BETA_FIRST = 0.9
BETA_SECOND = 0.999
ADAM_EPS = 1e-08
NORM_EPS = 1e-12


def layout():
    in_width = CODE + 3
    inner = H2 - CODE - 3
    shapes = [(in_width, inner), (H2, H2), (H2,), (inner,), (H2,), (inner,), (H2,), (1,)]
    pieces = []
    offset = 0
    for dims in shapes:
        entries = 1
        for extent in dims:
            entries = entries * extent
        pieces.append((offset, entries, dims))
        offset = offset + entries
    return pieces


def unpack(flat_all):
    return [
        flat_all[begin_at : begin_at + entries].reshape(dims)
        for begin_at, entries, dims in layout()
    ]


def effective(flat_all):
    first_dir, second_dir, head_vec, first_gain, second_gain, first_bias, second_bias, head_bias = (
        unpack(flat_all)
    )
    first_weight = first_dir * (
        first_gain * lax.rsqrt(jnp.sum(first_dir * first_dir, axis=0) + NORM_EPS)
    )
    second_weight = second_dir * (
        second_gain * lax.rsqrt(jnp.sum(second_dir * second_dir, axis=0) + NORM_EPS)
    )
    return (first_weight, second_weight, head_vec, first_bias, second_bias, head_bias)


def network(weights, point_codes, coord_rows):
    first_weight, second_weight, head_vec, first_bias, second_bias, head_bias = weights
    inputs = jnp.concatenate([point_codes, coord_rows], axis=1)
    first = jax.nn.silu(jnp.dot(inputs, first_weight, precision=PRECISE) + first_bias)
    joined = jnp.concatenate([first, inputs], axis=1)
    second = jax.nn.silu(jnp.dot(joined, second_weight, precision=PRECISE) + second_bias)
    return jnp.tanh(jnp.dot(second, head_vec, precision=PRECISE) + head_bias[0])


def shards(
    params,
    momentum,
    average,
    table,
    code_first,
    code_second,
    coords,
    targets,
    segment_ids,
    shape_code,
):
    rows_count = lax.axis_size("rows")
    mp_count = lax.axis_size("mp")
    device = lax.axis_index(("rows", "mp"))
    row_index = lax.axis_index("rows")
    mp_index = lax.axis_index("mp")
    points_here = segment_ids.shape[0]
    code_rows = table.shape[0]
    shapes_total = shape_code.shape[0]
    requests = SHAPES_DEV + 1
    chip_block = lax.all_gather(params, "mp", axis=0, tiled=True)
    flat_all = lax.all_gather(chip_block, "rows", axis=0, tiled=True)
    global_shape = jnp.max(segment_ids[: points_here // 16])
    local_ids = device * SHAPES_DEV + jnp.arange(SHAPES_DEV, dtype=jnp.int32)
    wanted = jnp.concatenate([global_shape[None], local_ids])
    all_wanted = lax.all_gather(wanted, ("rows", "mp"), axis=0, tiled=True)
    group_wanted = lax.dynamic_index_in_dim(
        all_wanted.reshape(rows_count, mp_count, requests), mp_index, 1, keepdims=False
    ).reshape(-1)
    shape_match = group_wanted[:, None] == jnp.arange(shapes_total, dtype=jnp.int32)[None, :]
    group_codes = jnp.sum(jnp.where(shape_match, shape_code[None, :], 0), axis=1)
    owned_local = group_codes - row_index * code_rows
    pick_mine = (owned_local[:, None] == jnp.arange(code_rows, dtype=jnp.int32)[None, :]).astype(
        jnp.float32
    )
    answer = jnp.dot(pick_mine, table, precision=PRECISE)
    codes_req = lax.psum_scatter(answer, "rows", scatter_dimension=0, tiled=True)
    is_valid = segment_ids >= 0
    valid_float = is_valid.astype(jnp.float32)
    slot_of = jnp.where(segment_ids == global_shape, 0, 1 + segment_ids - device * SHAPES_DEV)
    slot_hot = (slot_of[:, None] == jnp.arange(requests, dtype=jnp.int32)[None, :]).astype(
        jnp.float32
    )
    to_shapes = (wanted[:, None] == jnp.arange(shapes_total, dtype=jnp.int32)[None, :]).astype(
        jnp.float32
    )
    counts_dev = jnp.dot(
        jnp.dot(valid_float, slot_hot, precision=PRECISE), to_shapes, precision=PRECISE
    )
    counts_all = lax.psum(counts_dev, ("rows", "mp"))
    coord_rows = coords.T

    def local_net(flat_vals, code_vals):
        point_codes = jnp.dot(slot_hot, code_vals, precision=PRECISE)
        return network(effective(flat_vals), point_codes, coord_rows)

    predicted, pullback = jax.vjp(local_net, flat_all, codes_req)
    squash = jnp.tanh(predicted / CLAMP_DELTA)
    resid = CLAMP_DELTA * squash - CLAMP_DELTA * jnp.tanh(targets / CLAMP_DELTA)
    radius = jnp.sqrt(resid * resid + SMOOTH * SMOOTH)
    losses = jnp.where(is_valid, radius - SMOOTH, 0.0)
    loss_dev = jnp.dot(jnp.dot(losses, slot_hot, precision=PRECISE), to_shapes, precision=PRECISE)
    prior_mask = (jnp.arange(requests) > 0).astype(jnp.float32)[:, None]
    prior_dev = PRIOR_WEIGHT * jnp.sum(prior_mask * codes_req * codes_req)
    loss_tot, prior_tot = lax.psum((loss_dev, prior_dev), ("rows", "mp"))
    loss = (jnp.sum(loss_tot / counts_all) + prior_tot) / shapes_total
    count_point = jnp.dot(
        slot_hot, jnp.dot(to_shapes, counts_all, precision=PRECISE), precision=PRECISE
    )
    count_point = jnp.where(is_valid, count_point, 1.0)
    dpred = valid_float * (resid / radius) * (1.0 - squash * squash) / (count_point * shapes_total)
    grad_flat, grad_codes = pullback(dpred)
    grad_codes = grad_codes + 2.0 * PRIOR_WEIGHT / shapes_total * prior_mask * codes_req
    gathered = lax.all_gather(grad_codes, "rows", axis=0, tiled=True)
    table_part = jnp.dot(pick_mine.T, gathered, precision=PRECISE)
    grad_table = lax.psum(table_part, "mp")
    chip_grads = lax.psum_scatter(grad_flat, "rows", scatter_dimension=0, tiled=True)
    grad_shard = lax.psum_scatter(chip_grads, "mp", scatter_dimension=0, tiled=True)
    new_momentum = MOMENTUM_DECAY * momentum + grad_shard
    new_params = params - LEARN_RATE * (grad_shard + MOMENTUM_DECAY * new_momentum)
    new_average = AVERAGE_DECAY * average + (1.0 - AVERAGE_DECAY) * new_params
    owned_rows = shape_code - row_index * code_rows
    marks = jnp.sum(
        (owned_rows[:, None] == jnp.arange(code_rows, dtype=jnp.int32)[None, :]).astype(
            jnp.float32
        ),
        axis=0,
    )
    used_rows = marks[:, None] > 0.5
    first_new = BETA_FIRST * code_first + (1.0 - BETA_FIRST) * grad_table
    second_new = BETA_SECOND * code_second + (1.0 - BETA_SECOND) * grad_table * grad_table
    step_vals = (
        CODE_RATE
        * (first_new / (1.0 - BETA_FIRST**STEP))
        / (jnp.sqrt(second_new / (1.0 - BETA_SECOND**STEP)) + ADAM_EPS)
    )
    new_table = jnp.where(used_rows, table - step_vals, table)
    new_first = jnp.where(used_rows, first_new, code_first)
    new_second = jnp.where(used_rows, second_new, code_second)
    return (loss, new_momentum, new_params, new_average, new_table, new_first, new_second)


def solution(mesh):
    placed = (
        P(("rows", "mp")),
        P(("rows", "mp")),
        P(("rows", "mp")),
        P("rows", None),
        P("rows", None),
        P("rows", None),
        P(None, ("rows", "mp")),
        P(("rows", "mp")),
        P(("rows", "mp")),
        P(),
    )
    return jax.shard_map(
        shards,
        mesh=mesh,
        in_specs=placed,
        out_specs=(
            P(),
            P(("rows", "mp")),
            P(("rows", "mp")),
            P(("rows", "mp")),
            P("rows", None),
            P("rows", None),
            P("rows", None),
        ),
        check_vma=False,
    )
```

profile of v0, /device:TPU:0, one launch (start us, length us, event | category | flops | bytes accessed | tf_op | source)
XLA Modules:
  0.0 444.4 jit_solution(13617299169811597441)
XLA Ops:
  7.2 1.3 fusion.66
  9.2 1.2 dynamic-update-slice.1
  10.5 0.6 copy-done.9
  11.2 20.5 %all-reduce.20.cloned.1.call-done = f32[20608]{0:T(1024)} async-done(((f32[20608]{0:T(1024)}), f32[20608]{0:T(1024)}) %all-reduce.20.cloned.1.call-update) | async-done | bytes 82448
  31.7 1.6 reshape.77
  33.3 1.2 dynamic-slice.1
  35.9 1.3 slice_reduce_fusion
  37.2 0.8 fusion.64
  38.0 0.1 reshape.67
  38.2 40.9 %all-reduce.10 = s32[16,2,3]{2,1,0:T(2,128)S(1)} all-reduce(s32[16,2,3]{2,1,0:T(2,128)S(1)} %reshape.67), channel_id=1, replica_groups=mesh['rows'=16,'mp'=2] {'rows','mp'}, use_global_device_ids=true, to_apply=%add.8 | all-reduce | flops 96 | bytes 768
  79.1 0.1 eq.78
  79.2 0.8 select_reduce_fusion
  80.0 1.1 fusion.39
  81.1 75.9 %all-reduce.11 = f32[48,256]{1,0:T(8,128)S(1)} all-reduce(f32[48,256]{1,0:T(8,128)S(1)} %fusion.39), channel_id=2, replica_groups=mesh['rows'=16,'mp'=2] {'rows'}, use_global_device_ids=true, to_apply=%region_2.3.clone | all-reduce | flops 12288 | bytes 98304
  156.9 0.7 fusion.42
  158.3 0.7 broadcast_subtract_fusion
  158.9 1.4 subtract_select_fusion.1
  160.3 3.8 fusion.30
  164.1 1.3 slice.43
  165.4 1.0 slice.36
  166.3 1.6 slice.39
  167.9 0.4 reshape.68
  168.3 0.7 rsqrt_multiply_fusion.3
  169.1 0.2 reshape.69
  169.2 0.1 multiply_reduce_fusion.1
  169.4 0.8 fusion.65
  170.2 11.1 %fusion.9 = (f32[4096,253]{0,1:T(8,128)S(1)}, f32[4096,253]{0,1:T(8,128)}) fusion(f32[253]{0:T(256)S(1)} %get-tuple-element.29, f32[259,253]{1,0:T(8,128)S(1)} %reshape.68, f32[253]{0:T(256)S(1)} %get-tuple-element.28, f32[4096,3]{0,1:T(4,128)S(1)} %bitcast.58, f32[4096,256]{0,1:T(8,128)} %fusion.30), kind=kOutput, calls=%fused_computation.19 | convolution fusion | flops 3227090944 | bytes 12797892 | tf_op jit(solution)/shard_map/jvp()/dot_general | solution.py:64
  181.3 14.0 %fusion.4 = f32[4096,512]{1,0:T(8,128)S(1)} fusion(f32[4096,3]{0,1:T(4,128)S(1)} %bitcast.59, f32[4096,256]{0,1:T(8,128)S(1)} %copy-done.1, f32[4096,253]{0,1:T(8,128)S(1)} %get-tuple-element.39, f32[512,512]{1,0:T(8,128)S(1)} %reshape.69, f32[512]{0:T(512)S(1)} %get-tuple-element.27), kind=kOutput, calls=%fused_computation.10 | convolution fusion | flops 12889358336 | bytes 17827840 | tf_op jit(solution)/shard_map/jvp()/dot_general | solution.py:66
  195.4 8.8 %fusion.19 = f32[1,4096]{1,0:T(1,128)S(1)} fusion(f32[512,1]{0,1:T(1,128)S(1)} %bitcast.67, f32[4096,512]{1,0:T(8,128)S(1)} %fusion.4, f32[512]{0:T(512)S(1)} %get-tuple-element.25), kind=kOutput, calls=%fused_computation.37 | convolution fusion | flops 35651584 | bytes 8409088 | tf_op jit(solution)/shard_map/jvp()/dot_general | solution.py:67
  204.2 0.7 add_select_fusion
  204.9 0.2 convolution_bitcast_fusion.4
  205.2 0.2 convolution_bitcast_fusion.3
  205.3 0.2 convolution_bitcast_fusion.2
  205.5 0.2 convolution_bitcast_fusion.1
  205.7 36.8 %all-reduce.14 = (f32[64]{0:T(128)S(1)}, f32[64]{0:T(128)S(1)}, f32[]{:T(128)}) all-reduce(f32[64]{0:T(128)S(1)} %convolution_bitcast_fusion.2, f32[64]{0:T(128)S(1)} %convolution_bitcast_fusion.1, f32[]{:T(128)S(6)} %mul.265), channel_id=1, replica_groups=mesh['rows'=16,'mp'=2] {'rows','mp'}, use_global_device_ids=true, to_apply=%region_5.6 | all-reduce | flops 129 | bytes 1032 | tf_op jit(solution)/shard_map/psum | solution.py:135
  242.6 0.2 convolution_bitcast_fusion
  242.7 0.2 fusion.29
  243.0 1.3 fusion.59
  244.2 6.9 %fusion.60 = (f32[512]{0:T(512)S(1)}, f32[4096,512]{1,0:T(8,128)S(1)}) fusion(f32[4096,512]{1,0:T(8,128)} %copy-done.5, f32[512]{0:T(512)S(1)} %get-tuple-element.25, f32[512]{0:T(512)S(1)} %get-tuple-element.26, f32[4096]{0:T(1024)S(1)} %get-tuple-element.16), kind=kLoop, calls=%fused_computation.118 | loop fusion | flops 25165312 | bytes 16799744 | tf_op jit(solution)/shard_map/transpose(jvp())/reduce_sum | solution.py:66
  251.2 14.9 %multiply_reduce_fusion = (f32[512]{0:T(512)S(1)}, f32[512,512]{1,0:T(8,128)S(1)}) fusion(f32[512,512]{1,0:T(8,128)S(1)} %reshape.69, f32[4096,512]{1,0:T(8,128)S(1)} %get-tuple-element.18, f32[4096,3]{0,1:T(4,128)S(1)} %bitcast.60, f32[4096,256]{0,1:T(8,128)S(1)} %copy-done.2, f32[4096,253]{0,1:T(8,128)S(1)} %copy-done.8), kind=kOutput, calls=%fused_computation.31 | convolution fusion | flops 12889620480 | bytes 18876416 | tf_op jit(solution)/shard_map/transpose(jvp())/dot_general | solution.py:66
  266.1 13.7 %fusion.14 = f32[4096,512]{0,1:T(8,128)S(1)} fusion(f32[4096,512]{1,0:T(8,128)S(1)} %get-tuple-element.18, f32[512,512]{1,0:T(8,128)S(1)} %reshape.69, f32[512]{0:T(512)S(1)} %get-tuple-element.27), kind=kOutput, calls=%fused_computation.33 | convolution fusion | flops 12885164032 | bytes 17827840 | tf_op jit(solution)/shard_map/transpose(jvp())/dot_general | solution.py:66
  279.9 5.7 %fusion.17 = f32[1,512]{1,0:T(1,128)S(1)} fusion(f32[4096,1]{0,1:T(1,128)S(1)} %bitcast.64, f32[4096,512]{1,0:T(8,128)S(1)} %bitcast.49, f32[512]{0:T(512)S(1)} %get-tuple-element.25), kind=kOutput, calls=%fused_computation.36 | convolution fusion | flops 35651584 | bytes 8409088 | tf_op jit(solution)/shard_map/transpose(jvp())/dot_general | solution.py:67
  285.6 0.9 rsqrt_multiply_fusion
  286.5 0.2 fusion.13
  286.8 0.3 copy.25
  287.1 0.7 copy-done.6
  287.8 2.1 fusion.62
  289.9 3.6 multiply_reduce_fusion.2
  293.5 0.7 rsqrt_multiply_fusion.2
  294.3 0.4 reshape.71
  294.7 2.1 pad_add_fusion
  296.9 0.1 convert_reduce_fusion
  297.0 2.7 split.13
  299.7 0.8 copy-done.4
  300.4 4.1 fusion.23
  304.6 2.1 fusion.12
  306.7 39.7 %all-gather.1 = f32[16,3,256]{2,1,0:T(4,128)S(1)} all-gather(f32[1,3,256]{2,1,0:T(4,128)S(1)} %fusion.12), channel_id=1, replica_groups=mesh['rows'=16,'mp'=2] {'rows'}, dimensions={0}, use_global_device_ids=true | all-gather | bytes 52224 | tf_op jit(solution)/shard_map/all_gather | solution.py:144
  346.5 0.9 fusion.38
  347.4 65.6 %all-reduce.22.cloned.1.call-done = f32[329728]{0:T(1024)} async-done(((f32[329728]{0:T(1024)}), f32[329728]{0:T(1024)}) %all-reduce.22.cloned.1.call-update) | async-done | bytes 1318928
  413.0 1.6 dynamic-slice.4
  415.3 0.6 divide_reduce_fusion
  417.2 15.9 %all-reduce.24.cloned.1.call-done = (f32[20608]{0:T(1024)}, f32[64,256]{1,0:T(8,128)}) async-done(((f32[20608]{0:T(1024)}, f32[64,256]{1,0:T(8,128)}), (f32[20608]{0:T(1024)}, f32[64,256]{1,0:T(8,128)})) %all-reduce.24.cloned.1.call-update) | async-done | bytes 147984
  433.1 1.5 multiply_add_fusion.1
  434.7 1.6 fusion.32
  (61 shorter events, 0.6 us)
Async XLA Ops:
  7.2 24.5 %all-reduce.20.cloned.1.call-start = ((), (), s32[]{:S(2)}) async-start(), calls=%async_computation | async-start | bytes 172032
  10.5 0.6 copy-start.9
  11.1 153.0 %all-gather.4.cloned.1.call-start = ((), (), s32[]{:S(2)}) async-start(), calls=%async_computation.1 | async-start | bytes 1401344 | tf_op jit(solution)/shard_map/all_gather | solution.py:92
  33.3 379.7 %all-reduce.22.cloned.1.call-start = ((), (), s32[]{:S(2)}) async-start(), calls=%async_computation.2 | async-start | bytes 2637824
  164.1 6.1 %copy-start.10 = (f32[3,4096]{1,0:T(4,128)S(1)}, f32[3,4096]{1,0:T(4,128)}, u32[]{:S(2)}) copy-start(f32[3,4096]{1,0:T(4,128)} %param.16) | copy-start | bytes 147460
  170.2 11.1 %copy-start.1 = (f32[4096,256]{0,1:T(8,128)S(1)}, f32[4096,256]{0,1:T(8,128)}, u32[]{:S(2)}) copy-start(f32[4096,256]{0,1:T(8,128)} %fusion.30) | copy-start | bytes 12582916
  181.3 14.0 %copy-start.7 = (f32[4096,253]{0,1:T(8,128)}, f32[4096,253]{0,1:T(8,128)S(1)}, u32[]{:S(2)}) copy-start(f32[4096,253]{0,1:T(8,128)S(1)} %get-tuple-element.39) | copy-start | bytes 12435460
  195.3 8.9 %copy-start.5 = (f32[4096,512]{1,0:T(8,128)}, f32[4096,512]{1,0:T(8,128)S(1)}, u32[]{:S(2)}) copy-start(f32[4096,512]{1,0:T(8,128)S(1)} %fusion.4) | copy-start | bytes 25165828
  195.3 8.9 %copy-start.13 = (f32[4096]{0:T(1024)S(1)}, f32[4096]{0:T(1024)}, u32[]{:S(2)}) copy-start(f32[4096]{0:T(1024)} %param.17) | copy-start | bytes 49156
  195.3 8.9 %copy-start.14 = (s32[4096]{0:T(1024)S(1)}, s32[4096]{0:T(1024)}, u32[]{:S(2)}) copy-start(s32[4096]{0:T(1024)} %param.18) | copy-start | bytes 49156
  244.2 6.9 %copy-start.2 = (f32[4096,256]{0,1:T(8,128)S(1)}, f32[4096,256]{0,1:T(8,128)}, u32[]{:S(2)}) copy-start(f32[4096,256]{0,1:T(8,128)} %fusion.30) | copy-start | bytes 12582916
  244.2 6.9 %copy-start.8 = (f32[4096,253]{0,1:T(8,128)S(1)}, f32[4096,253]{0,1:T(8,128)}, u32[]{:S(2)}) copy-start(f32[4096,253]{0,1:T(8,128)} %copy-done.7) | copy-start | bytes 12435460
  251.1 28.7 %slice-start = ((s8[8388608]{0:T(1024)(128)(4,1)}), s8[4194304]{0:T(1024)(128)(4,1)S(1)}, s32[]{:S(2)}) async-start(s8[8388608]{0:T(1024)(128)(4,1)} %bitcast.48), calls=%async_computation.4 | async-start | bytes 8388608
  266.1 13.8 %slice-start.1 = ((s8[8388608]{0:T(1024)(128)(4,1)}), s8[4194304]{0:T(1024)(128)(4,1)S(1)}, s32[]{:S(2)}) async-start(s8[8388608]{0:T(1024)(128)(4,1)} %bitcast.48), calls=%async_computation.5 | async-start | bytes 8388608
  279.9 7.2 %copy-start = (f32[4096,512]{0,1:T(8,128)}, f32[4096,512]{0,1:T(8,128)S(1)}, u32[]{:S(2)}) copy-start(f32[4096,512]{0,1:T(8,128)S(1)} %fusion.14) | copy-start | bytes 25165828
  285.6 2.2 copy-start.6
  289.9 3.6 copy-start.3
  296.8 136.3 %all-reduce.24.cloned.1.call-start = ((), (), s32[]{:S(2)}) async-start(), calls=%async_computation.3 | async-start | bytes 303104
  297.0 3.5 copy-start.4
  304.5 128.6 %copy-start.12 = (f32[10304]{0:T(1024)S(1)}, f32[10304]{0:T(1024)}, u32[]{:S(2)}) copy-start(f32[10304]{0:T(1024)} %param.10) | copy-start | bytes 123652
  304.5 128.6 %copy-start.17 = (f32[10304]{0:T(1024)S(1)}, f32[10304]{0:T(1024)}, u32[]{:S(2)}) copy-start(f32[10304]{0:T(1024)} %param.12) | copy-start | bytes 123652
  304.6 128.6 %copy-start.18 = (f32[10304]{0:T(1024)S(1)}, f32[10304]{0:T(1024)}, u32[]{:S(2)}) copy-start(f32[10304]{0:T(1024)} %param.11) | copy-start | bytes 123652
  304.6 130.1 %copy-start.11 = (f32[64,256]{1,0:T(8,128)S(1)}, f32[64,256]{1,0:T(8,128)}, u32[]{:S(2)}) copy-start(f32[64,256]{1,0:T(8,128)} %param.13) | copy-start | bytes 196612
  304.6 130.1 %copy-start.15 = (f32[64,256]{1,0:T(8,128)S(1)}, f32[64,256]{1,0:T(8,128)}, u32[]{:S(2)}) copy-start(f32[64,256]{1,0:T(8,128)} %param.15) | copy-start | bytes 196612
  304.6 130.1 %copy-start.16 = (f32[64,256]{1,0:T(8,128)S(1)}, f32[64,256]{1,0:T(8,128)}, u32[]{:S(2)}) copy-start(f32[64,256]{1,0:T(8,128)} %param.14) | copy-start | bytes 196612
Sparse Core Ops, SparseCore 0:
  11.2 20.3 all-reduce.19
  34.5 58.3 all-gather.3
  296.9 116.0 all-reduce.21
  415.9 17.1 all-reduce.23
where the time goes:
time: 452 us; the launch traced here: 444 us
  blocking collectives  193 us (43%)
  waiting for transfers between devices  102 us (23%)
  matrix products  85 us (19%)
  other arithmetic  26.2 us (6%)
  between operations  20.3 us (4%)
  local copies, waits for them, and re-layouts  17.2 us (4%)
    unnamed x2, blocking collectives  117 us
    unnamed x7, waiting for transfers between devices  102 us
    dot_general x3, matrix products, network(): jnp.dot(joined, second_weight, precision=PRECISE) + second_bias  42.6 us
    all_gather x1, blocking collectives, shards(): gathered = lax.all_gather(grad_codes, 'rows', axis=0, tiled=True)  39.7 us
    psum x1, blocking collectives, shards(): loss_tot, prior_tot = lax.psum((loss_dev, prior_dev), ('rows', 'mp'))  36.8 us
    dot_general x3, matrix products, network(): jnp.dot(inputs, first_weight, precision=PRECISE) + first_bias  18.8 us
    dot_general x2, matrix products, network(): return jnp.tanh(jnp.dot(second, head_vec, precision=PRECISE) + head_bias[0])  14.5 us
    unnamed x51, local copies, waits for them, and re-layouts  9.51 us
  transfers between devices with their start and end apart: 4, of which 3 were waited for; matrix products, arithmetic and copies ran while one was open for 5% of the time, Pallas kernels for 0%

commit v1 on v0

v1 whole, which is shorter than its diff:
```python
import functools
import math

import jax
import jax.numpy as jnp
from jax import lax
from jax.experimental import pallas as pl
from jax.experimental.pallas import tpu as pltpu
from jax.sharding import PartitionSpec as P

MESH = pl.DeviceIdType.MESH
F32, BF16 = jnp.float32, jnp.bfloat16
EXACT = lax.Precision.HIGHEST
CODE = 256
H2 = 512
INNER = H2 - CODE - 3
STEP = 10
CLAMP_DELTA = 0.1
SMOOTH = 0.01
PRIOR_WEIGHT = 0.001
LEARN_RATE = 200.0
MOMENTUM_DECAY = 0.9
AVERAGE_DECAY = 0.9
CODE_RATE = 0.5
BETA_FIRST = 0.9
BETA_SECOND = 0.999
ADAM_EPS = 1e-08
NORM_EPS = 1e-12
LANES = 128

SECOND_AT = (CODE + 3) * INNER
SECOND_ROW, SHIFT = divmod(SECOND_AT, LANES)
TAIL_AT = SECOND_AT + H2 * H2 + H2
TAIL_ROW = TAIL_AT // LANES
TAIL_PIECES = (INNER, H2, INNER, H2, 1)


def chip_dims(rows):
    return {16: (4, 2, 2), 128: (4, 4, 8)}.get(rows, (rows, 1, 1))


def piece_rows(per_device, devices):
    most = max((per_device * d) % LANES for d in range(devices))
    rows = -(-(most + per_device) // LANES)
    return rows, (rows // 8 + 1) * 8


class Place:
    def __init__(self, dims):
        self.dims = dims
        self.row = lax.axis_index("rows")
        self.core = lax.axis_index("mp")
        d0, d1, d2 = dims
        self.at = [self.row // (d1 * d2), (self.row // d2) % d1, self.row % d2]

    def peer(self, dim, step):
        at = list(self.at)
        at[dim] = (at[dim] + step) % self.dims[dim]
        d0, d1, d2 = self.dims
        return at[dim], ((at[0] * d1 + at[1]) * d2 + at[2], self.core)

    def sibling(self):
        return (self.row, 1 - self.core)

    def steps(self, dim):
        return range(1, self.dims[dim])


def remote(src, dst, send, recv, device):
    return pltpu.make_async_remote_copy(
        src, dst, send, recv, device_id=device, device_id_type=MESH
    )


class Gather:
    def __init__(self, place, buf, chunks, orders, send, recv):
        self.p, self.buf, self.chunks, self.orders = place, buf, chunks, orders
        self.send, self.recv, self.live = send, recv, {}

    def view(self, done, core, k):
        idx = [slice(None) if d in done else self.p.at[d] for d in range(3)]
        begin, size = self.chunks[k]
        return self.buf.at[core, idx[0], idx[1], idx[2], pl.ds(begin, size)]

    def start(self, k, stage):
        order = self.orders[k % len(self.orders)]
        core = self.p.core
        copies = []
        if stage == 3:
            v = self.view(order, core, k)
            copies.append(remote(v, v, self.send.at[k, 3, 0], self.recv.at[k, 3, 0], self.p.sibling()))
        else:
            for o in self.p.steps(order[stage]):
                v = self.view(order[:stage], core, k)
                dev = self.p.peer(order[stage], o)[1]
                copies.append(remote(v, v, self.send.at[k, stage, o], self.recv.at[k, stage, o], dev))
        for c in copies:
            c.start()
        self.live[k, stage] = copies

    def arrive(self, k, stage):
        for c in self.live[k, stage]:
            c.wait_recv()

    def finish(self):
        for copies in self.live.values():
            for c in copies:
                c.wait_send()


class Reduce:
    def __init__(self, place, buf, landing, chunks, orders, send, recv, cores):
        self.p, self.buf, self.landing, self.chunks, self.orders = place, buf, landing, chunks, orders
        self.send, self.recv, self.cores, self.live = send, recv, cores, {}

    def index(self, k, stage, last):
        order = self.orders[k % len(self.orders)]
        idx = [self.p.at[d] if d in order[:stage] else slice(None) for d in range(3)]
        if last is not None:
            idx[order[stage]] = last
        begin, size = self.chunks[k]
        return tuple(idx) + (pl.ds(begin, size),)

    def landed(self, k, stage, o):
        ref = self.landing[1 + 3 * (k % len(self.orders)) + stage]
        begin, size = self.chunks[k]
        return ref.at[(o - 1,) + (slice(None),) * (2 - stage) + (pl.ds(begin, size),)]

    def start(self, k, stage):
        order = self.orders[k % len(self.orders)]
        copies = []
        if stage < 0:
            idx = self.index(k, 0, None)
            copies.append(
                remote(
                    self.buf.at[(1 - self.p.core,) + idx],
                    self.landing[0].at[idx],
                    self.send.at[k, 3, 0],
                    self.recv.at[k, 3, 0],
                    self.p.sibling(),
                )
            )
        else:
            for o in self.p.steps(order[stage]):
                at, dev = self.p.peer(order[stage], o)
                idx = self.index(k, stage, at)
                copies.append(
                    remote(
                        self.buf.at[(self.p.core,) + idx],
                        self.landed(k, stage, o),
                        self.send.at[k, stage, o],
                        self.recv.at[k, stage, o],
                        dev,
                    )
                )
        for c in copies:
            c.start()
        self.live[k, stage] = copies

    def arrive(self, k, stage):
        for c in self.live[k, stage]:
            c.wait_recv()
        order = self.orders[k % len(self.orders)]
        if stage < 0:
            idx = self.index(k, 0, None)
            mine = (self.p.core,) + idx
            self.buf[mine] = self.buf[mine] + self.landing[0][idx]
        else:
            idx = self.index(k, stage, self.p.at[order[stage]])
            mine = (self.p.core,) + idx
            total = self.buf[mine]
            for o in self.p.steps(order[stage]):
                total = total + self.landed(k, stage, o)[...]
            self.buf[mine] = total

    def finish(self):
        for copies in self.live.values():
            for c in copies:
                c.wait_send()


def landings(dims, orders, tail):
    shapes = [tuple(dims) + tail]
    for order in orders:
        for stage, d in enumerate(order):
            rest = tuple(dims[e] for e in range(3) if e not in order[: stage + 1])
            shapes.append((max(dims[d] - 1, 1),) + rest + tail)
    return [pltpu.VMEM(shape, F32) for shape in shapes]


def iota(shape, dim):
    return lax.broadcasted_iota(jnp.int32, shape, dim)


def dot(a, b, precision=None):
    return jnp.dot(a, b, precision=precision, preferred_element_type=F32)


def dot_nt(a, b, precision=None):
    return lax.dot_general(
        a, b, (((1,), (1,)), ((), ())), precision=precision, preferred_element_type=F32
    )


def dot_tn(a, b, precision=None):
    return lax.dot_general(
        a, b, (((0,), (0,)), ((), ())), precision=precision, preferred_element_type=F32
    )


def turn(x, by):
    by = by % x.shape[1]
    return pltpu.roll(x, by, 1) if by else x


def widen(x, width):
    return jnp.concatenate([x, jnp.zeros((x.shape[0], width - x.shape[1]), F32)], axis=1)


def one_row(x, count):
    return jnp.concatenate([x[k : k + 1] for k in range(count)], axis=1)


def bounds(devices, per_device):
    for d in range(devices):
        row, phase = divmod(per_device * d, LANES)
        yield d, row, phase, -(-(phase + per_device) // LANES)


def assemble(dims, per_device, buf, flat):
    rows = dims[0] * dims[1] * dims[2]
    for d, row, phase, count in bounds(2 * rows, per_device):
        chip = d // 2
        src = buf.at[d % 2, chip // (dims[1] * dims[2]), (chip // dims[2]) % dims[1], chip % dims[2]]
        if phase:
            flat[row : row + 1, :] = flat[row : row + 1, :] + src[0:1, :]
            flat[row + 1 : row + count, :] = src[1:count, :]
        else:
            flat[row : row + count, :] = src[0:count, :]


def scatter(dims, per_device, rows_kept, flat, buf):
    rows = dims[0] * dims[1] * dims[2]
    for d, row, phase, count in bounds(2 * rows, per_device):
        chip = d // 2
        dst = buf.at[d % 2, chip // (dims[1] * dims[2]), (chip // dims[2]) % dims[1], chip % dims[2]]
        dst[...] = flat[row : row + rows_kept, :]


def first_blocks():
    for back in range(4):
        begin = -(-256 * back // 3)
        end = min(-(-256 * (back + 1) // 3), CODE + 3)
        for at in range(begin, end, 8):
            yield back, at, min(8, end - at)


def unpack_first(flat, wide, v1):
    wide[0:8, :] = jnp.zeros((8, 256), F32)
    for half in range(2):
        lanes = slice(half * LANES, (half + 1) * LANES)
        wide[8:272, lanes] = flat[pl.ds(half, 264, stride=2), :]
    v1[256:264, :] = jnp.zeros((8, 256), F32)
    for back, at, n in first_blocks():
        base = 3 * at - 256 * back
        lane = iota((n, 256), 1)
        move = base + 3 * iota((n, 256), 0)
        here = wide[8 + at - back : 8 + at - back + n, :]
        before = wide[7 + at - back : 7 + at - back + n, :]
        mixed = jnp.where(lane < 256 - move, here, before)
        mixed = turn(mixed, base)
        if n > 1:
            mixed = pltpu.roll(mixed, 0, 1, stride=3, stride_axis=0)
        v1[at : at + n, :] = jnp.where(lane < INNER, mixed, 0.0)


def pack_first(v1, wide, flat):
    wide[...] = jnp.zeros(wide.shape, F32)
    for back, at, n in first_blocks():
        base = 3 * at - 256 * back
        lane = iota((n, 256), 1)
        sub = iota((n, 256), 0)
        moved = turn(v1[at : at + n, :], -base)
        for bit in range(3):
            moved = jnp.where((sub >> bit) & 1 == 1, turn(moved, -3 * (1 << bit)), moved)
        here = lane < 256 - (base + 3 * sub)
        a = slice(8 + at - back, 8 + at - back + n)
        b = slice(7 + at - back, 7 + at - back + n)
        wide[a, :] = wide[a, :] + jnp.where(here, moved, 0.0)
        wide[b, :] = wide[b, :] + jnp.where(here, 0.0, moved)
    for half in range(2):
        lanes = slice(half * LANES, (half + 1) * LANES)
        flat[pl.ds(half, 256, stride=2), :] = wide[8:264, lanes]


def unpack_second(flat, v2):
    for q in range(H2 // LANES):
        lanes = slice(q * LANES, (q + 1) * LANES)
        for at in range(0, H2 + 8, 104):
            rows = flat[pl.ds(SECOND_ROW + q + 4 * at, 104, stride=4), :]
            if q == 0:
                after = flat[pl.ds(SECOND_ROW + 4 + 4 * at, 104, stride=4), :]
                rows = jnp.where(iota((104, LANES), 1) < SHIFT, after, rows)
            v2[at : at + 104, lanes] = rows


def pack_second(v2, flat):
    low = iota((1, LANES), 1) < SHIFT
    for q in range(1, H2 // LANES):
        lanes = slice(q * LANES, (q + 1) * LANES)
        flat[pl.ds(SECOND_ROW + q, H2, stride=4), :] = v2[0:H2, lanes]
        flat[SECOND_ROW + q + 4 * H2 : SECOND_ROW + q + 4 * H2 + 1, :] = v2[H2 : H2 + 1, lanes]
    flat[pl.ds(SECOND_ROW + 4, H2, stride=4), :] = jnp.where(low, v2[0:H2, 0:LANES], v2[1 : H2 + 1, 0:LANES])
    flat[SECOND_ROW : SECOND_ROW + 1, :] = jnp.where(
        low, flat[SECOND_ROW : SECOND_ROW + 1, :], v2[0:1, 0:LANES]
    )
    flat[TAIL_ROW : TAIL_ROW + 1, :] = jnp.where(low, v2[H2 : H2 + 1, 0:LANES], 0.0)


def unpack_tail(flat):
    count = 13
    tail = one_row(flat[TAIL_ROW : TAIL_ROW + count, :], count)
    at = SHIFT
    parts = []
    for width in TAIL_PIECES:
        lanes = {INNER: 256, H2: H2, 1: LANES}[width]
        piece = turn(tail, -at)[:, 0:lanes]
        if width == H2:
            piece = turn(piece, SHIFT)
        else:
            piece = jnp.where(iota((1, lanes), 1) < width, piece, 0.0)
        parts.append(piece)
        at += width
    return parts


def pack_tail(parts, flat):
    count = 13
    at = SHIFT
    total = jnp.zeros((1, count * LANES), F32)
    for width, piece in zip(TAIL_PIECES, parts):
        if width == H2:
            piece = turn(piece, -SHIFT)
        else:
            piece = jnp.where(iota(piece.shape, 1) < width, piece, 0.0)
        total = total + turn(widen(piece, count * LANES), at)
        at += width
    flat[TAIL_ROW : TAIL_ROW + 1, :] = flat[TAIL_ROW : TAIL_ROW + 1, :] + total[:, 0:LANES]
    for k in range(1, count):
        flat[TAIL_ROW + k : TAIL_ROW + k + 1, :] = total[:, k * LANES : (k + 1) * LANES]


def split2(x):
    high = x.astype(BF16)
    return high, (x - high.astype(F32)).astype(BF16)


def split3(x):
    a = x.astype(BF16).astype(F32)
    b = (x - a).astype(BF16).astype(F32)
    return a, b, x - a - b


def kernel(
    cfg,
    piece_ref,
    table_ref,
    code_first_ref,
    code_second_ref,
    coords_ref,
    targets_ref,
    seg_ref,
    shape_code_ref,
    loss_ref,
    grad_ref,
    new_table_ref,
    new_first_ref,
    new_second_ref,
    buf,
    landing,
    flat,
    wide,
    v1,
    v2,
    g1,
    g2,
    w2t,
    w2b,
    w0,
    bias,
    head,
    points,
    hc,
    h1,
    slope1,
    h2,
    act,
    second,
    d2b,
    df,
    d1b,
    dw2,
    dw1,
    dhead,
    sums,
    codes_buf,
    codes_landing,
    grads_buf,
    psend,
    precv,
    csend,
    crecv,
    dsend,
    drecv,
    rsend,
    rrecv,
):
    dims, per_device, tile = cfg["dims"], cfg["per_device"], cfg["tile"]
    used, kept = piece_rows(per_device, 2 * cfg["rows"])
    rows = cfg["rows"]
    shapes = cfg["shapes"]
    place = Place(dims)
    device = place.row * 2 + place.core
    tiles = seg_ref.shape[0] * LANES // tile
    per_tile = tile // LANES
    head_len = seg_ref.shape[0] * LANES // 16

    barrier = pltpu.get_barrier_semaphore()
    greeted = 1
    pl.semaphore_signal(barrier, inc=1, device_id=place.sibling(), device_id_type=MESH)
    for dim in range(3):
        for o in place.steps(dim):
            pl.semaphore_signal(barrier, inc=1, device_id=place.peer(dim, o)[1], device_id_type=MESH)
            greeted += 1
    pl.semaphore_wait(barrier, greeted)

    seg_heads = seg_ref[0 : head_len // LANES, :].astype(F32)
    shared = jnp.max(jnp.max(seg_heads, axis=1, keepdims=True), axis=0, keepdims=True)
    for q in range(per_tile):
        lanes = slice(q * LANES, (q + 1) * LANES)
        points[0, :, lanes] = seg_ref[pl.ds(q, tiles, stride=per_tile), :].astype(F32)
        points[1, :, lanes] = jnp.tanh(targets_ref[pl.ds(q, tiles, stride=per_tile), :] * (1.0 / CLAMP_DELTA))
    seg = points[0]

    def count(where):
        return jnp.sum(jnp.sum(where.astype(F32), axis=1, keepdims=True), axis=0, keepdims=True)

    mine = (device * 2).astype(F32)
    counts = [count(seg == shared), count(seg == mine), count(seg == mine + 1.0)]

    own = buf.at[place.core, place.at[0], place.at[1], place.at[2]]
    own[0 : kept - 8, :] = piece_ref[0 : kept - 8, :]
    own[kept - 8 : kept, :] = jnp.where(
        iota((8, LANES), 0) == 7, jnp.broadcast_to(counts[0], (8, LANES)), piece_ref[kept - 8 : kept, :]
    )

    gather = Gather(place, buf, cfg["chunks"], cfg["gather_orders"], psend, precv)
    chunk_ids = range(len(cfg["chunks"]))
    for k in chunk_ids:
        gather.start(k, 0)

    base = (place.row * table_ref.shape[0]).astype(F32)
    codes_of = jnp.broadcast_to(shape_code_ref[...].astype(F32) + 1.0, (8, shapes))
    slots = rows * 8
    kind = iota((slots, shapes), 0) & 7
    owner = (iota((slots, shapes), 0) >> 3) * 2 + place.core
    shape_id = iota((slots, shapes), 1)
    asked = jnp.where(
        kind == 3,
        (shape_id.astype(F32) == shared).astype(F32),
        jnp.where((kind == 4) | (kind == 5), (shape_id == owner * 2 + kind - 4).astype(F32), 0.0),
    )
    wanted = dot_nt(asked, codes_of, EXACT)[:, 0:1] - 1.0 - base
    pick = (wanted == iota((slots, table_ref.shape[0]), 1).astype(F32)).astype(F32)
    answer = dot(pick, table_ref[...], EXACT)
    codes_buf[place.core] = answer.reshape(dims + (8, CODE))
    codes = Reduce(place, codes_buf, codes_landing, [(0, 8)], [(2, 1, 0)], csend, crecv, False)
    codes.start(0, 0)

    for stage in range(4):
        if stage < 3:
            codes.arrive(0, stage)
            if stage < 2:
                codes.start(0, stage + 1)
        for k in chunk_ids:
            gather.arrive(k, stage)
            if stage < 3:
                gather.start(k, stage + 1)
    z8 = codes_buf[place.core, place.at[0], place.at[1], place.at[2]]

    assemble(dims, per_device, buf, flat)
    unpack_first(flat, wide, v1)
    unpack_second(flat, v2)
    gain1, gain2, bias1, bias2, head_bias = unpack_tail(flat)
    norm1 = jnp.sum(v1[...] * v1[...], axis=0, keepdims=True) + NORM_EPS
    norm2 = jnp.sum(v2[0:H2, :] * v2[0:H2, :], axis=0, keepdims=True) + NORM_EPS
    inv1, inv2 = lax.rsqrt(norm1), lax.rsqrt(norm2)
    scale1, scale2 = gain1 * inv1, gain2 * inv2
    head_row = v2[H2 : H2 + 1, :]
    hbias = head_bias[:, 0:1]

    total = jnp.sum(buf[:, :, :, :, kept - 8 : kept, :], axis=(0, 1, 2, 3))[7:8, 0:1]
    counts_all = [total]
    for k in (1, 2):
        counts_all.append(jnp.where(shared == mine + (k - 1.0), total, jnp.maximum(counts[k], 1.0)))
    inv_counts = [1.0 / (n * float(shapes)) for n in counts_all]
    position = iota((tiles, tile), 0) * tile + iota((tiles, tile), 1)
    is_two = (seg == mine + 1.0) & (position >= head_len)
    per_point = jnp.where(
        position < head_len, inv_counts[0], jnp.where(is_two, inv_counts[2], inv_counts[1])
    )
    points[2] = jnp.where(seg >= 0.0, per_point, 0.0)
    points[3] = jnp.where(is_two, 1.0, 0.0)

    lane1 = iota((8, 256), 1)
    sub1 = iota((8, 256), 0)
    code1 = dot(z8, v1[0:CODE, :], EXACT) * scale1 + bias1
    xyz1 = v1[CODE : CODE + 8, :] * scale1
    rows1 = 0.5 * jnp.where(sub1 < 3, xyz1, jnp.where(sub1 < 6, code1, 0.0))
    rows1 = jnp.where(lane1 < INNER, rows1, (lane1 == INNER + sub1).astype(F32))
    rows1 = jnp.where(sub1 < 6, rows1, 0.0)
    wa, wb, wc = split3(rows1)
    stack = jnp.concatenate([wa, wa, wb, wb, wa, wc] + [jnp.zeros((8, 256), F32)] * 10, axis=0)
    w0[...] = stack.T.astype(BF16)

    z_wide = turn(widen(z8, H2), INNER)
    code2 = 0.5 * (dot(z_wide, v2[0:H2, :], EXACT) * scale2 + bias2)
    sub2 = iota((8, H2), 0)
    columns = jnp.where(sub2 == 6, jnp.broadcast_to(0.5 * head_row, (8, H2)), code2)
    columns = jnp.concatenate([columns, jnp.zeros((LANES - 8, H2), F32)], axis=0).T
    for k in range(3):
        bias[k] = jnp.broadcast_to(columns[:, 3 + k : 4 + k], (H2, LANES))
    head[...] = jnp.broadcast_to(columns[:, 6:7], (H2, LANES))
    xyz2 = pltpu.roll(v2[H2 - 8 : H2, :], 0, 0)
    last = jnp.where(iota((8, H2), 0) < 5, v2[248:256, :], xyz2)
    normal = jnp.concatenate([v2[0:248, :], last], axis=0) * scale2
    w2b[...] = normal.astype(BF16)
    high, low = split2(0.5 * normal.T)
    w2t[:, 0:256] = high
    w2t[:, 256:512] = high
    w2t[:, 512:768] = low

    dw2[...] = jnp.zeros(dw2.shape, F32)
    dw1[...] = jnp.zeros(dw1.shape, F32)
    dhead[...] = jnp.zeros(dhead.shape, F32)
    sums[...] = jnp.zeros(sums.shape, F32)
    block = 32

    def one_tile(t, _):
        at = pl.ds(pl.multiple_of(t * tile, tile), tile)
        two = points[3, pl.ds(t, 1), :]
        here = t * tile + iota((1, tile), 1)
        is_head = (here < head_len).astype(F32)
        one = 1.0 - two - is_head
        x8 = jnp.concatenate(
            [coords_ref[:, at], is_head, one, two, jnp.zeros((2, tile), F32)], axis=0
        )
        xa, xb, xc = split3(x8)
        x48 = jnp.concatenate([xa, xb, xa, xb, xc, xa], axis=0).astype(BF16)
        hc[768:784, :] = jnp.concatenate([xa, xb], axis=0).astype(BF16)
        h1[...] = dot(w0[:, 0:48], x48)
        for u in range(0, 256, block):
            for q in range(per_tile):
                lanes = slice(q * LANES, (q + 1) * LANES)
                us = slice(u, u + block)
                h = h1[us, lanes]
                th = jnp.tanh(h)
                m = h * th
                f = h + m
                slope1[us, lanes] = (0.5 + 0.5 * th) * (1.0 + (h - m))
                if u + block > INNER:
                    f = jnp.where(iota((block, LANES), 0) + u >= INNER, h, f)
                fh, fl = split2(f)
                hc[us, lanes] = fh
                hc[256 + u : 256 + u + block, lanes] = fl
                hc[512 + u : 512 + u + block, lanes] = fh
        h2[...] = dot(w2t[...], hc[0:768, :])
        parts = []
        for q in range(per_tile):
            lanes = slice(q * LANES, (q + 1) * LANES)
            in_head = t * per_tile + q < head_len // LANES
            b_one = jnp.where(in_head, 0, 1)
            b_two = jnp.where(in_head, 0, 2)
            is_second = jnp.broadcast_to(two[:, lanes], (block, LANES)) > 0.5
            part = jnp.zeros((8, LANES), F32)
            for u in range(0, H2, block):
                us = slice(u, u + block)
                h = h2[us, lanes] + jnp.where(is_second, bias[b_two, us, :], bias[b_one, us, :])
                th = jnp.tanh(h)
                m = h * th
                s = h + m
                hw = head[us, :]
                second[us, lanes] = s
                act[us, lanes] = hw * ((1.0 + th) * (1.0 + (h - m)))
                w = hw * s
                for v in range(0, block, 8):
                    part = part + w[v : v + 8]
            parts.append(jnp.sum(part, axis=0, keepdims=True))
        raw = 2.0 * jnp.concatenate(parts, axis=1) + hbias
        pred = jnp.tanh(raw)
        squash = jnp.tanh(pred * (1.0 / CLAMP_DELTA))
        resid = CLAMP_DELTA * squash - CLAMP_DELTA * points[1, pl.ds(t, 1), :]
        square = resid * resid + SMOOTH * SMOOTH
        inv_radius = lax.rsqrt(square)
        share = points[2, pl.ds(t, 1), :]
        dpred = share * (resid * inv_radius) * (1.0 - squash * squash) * (1.0 - pred * pred)
        sums[0:1, :] = sums[0:1, :] + share * (square * inv_radius - SMOOTH)
        sums[1:2, :] = sums[1:2, :] + dpred
        for u in range(0, H2, block):
            us = slice(u, u + block)
            total_u = dhead[us, :]
            for q in range(per_tile):
                lanes = slice(q * LANES, (q + 1) * LANES)
                dp = jnp.broadcast_to(dpred[:, lanes], (block, LANES))
                d2b[us, lanes] = (act[us, lanes] * dp).astype(BF16)
                total_u = total_u + second[us, lanes] * dp
            dhead[us, :] = total_u
        df[...] = dot(w2b[...], d2b[...])
        dw2[...] = dw2[...] + dot_nt(hc[512:784, :], d2b[...])
        for u in range(0, 256, block):
            us = slice(u, u + block)
            d1b[us, :] = (df[us, :] * slope1[us, :]).astype(BF16)
        dw1[...] = dw1[...] + dot_nt(hc[768:784, :], d1b[...])
        return 0

    lax.fori_loop(0, tiles, one_tile, 0)

    outer1 = jnp.where(lane1 < INNER, dw1[0:8, :] + dw1[8:16, :], 0.0)
    outer2 = dw2[256:264, :] + dw2[264:272, :]
    slot_rows = (sub1 >= 3) & (sub1 < 6)
    d1 = jnp.where(slot_rows, outer1, 0.0)
    d2 = jnp.where((sub2 >= 3) & (sub2 < 6), outer2, 0.0)
    dz = dot_nt(d1 * scale1, v1[0:CODE, :], EXACT)
    dz = dz + turn(dot_nt(d2 * scale2, v2[0:H2, :], EXACT), -INNER)[:, 0:CODE]
    own_rows = (sub1 == 4) | (sub1 == 5)
    dz = dz + jnp.where(own_rows, (2.0 * PRIOR_WEIGHT / shapes) * z8, 0.0)
    prior = jnp.where(own_rows, z8 * z8, 0.0)
    prior = (PRIOR_WEIGHT / shapes) * jnp.sum(jnp.sum(prior, axis=1, keepdims=True), axis=0, keepdims=True)
    loss_here = jnp.sum(sums[0:1, :], axis=1, keepdims=True) + prior
    message = jnp.where(slot_rows, dz, 0.0)
    message = jnp.where(sub1 == 0, jnp.broadcast_to(loss_here, (8, CODE)), message)
    grads_buf[place.core, place.at[0], place.at[1], place.at[2]] = message
    spread = Gather(place, grads_buf, [(0, 8)], [(0, 1, 2)], dsend, drecv)
    spread.start(0, 0)

    g1[0:CODE, :] = dot_tn(z8, d1, EXACT)
    g1[CODE : CODE + 8, :] = jnp.where(sub1 < 3, outer1, 0.0)
    along1 = jnp.sum(v1[...] * g1[...], axis=0, keepdims=True)
    g1[...] = g1[...] * scale1 - v1[...] * (scale1 * inv1 * inv1 * along1)
    g2[0:H2, :] = dot_tn(z_wide, d2, EXACT)
    g2[0:256, :] = g2[0:256, :] + jnp.where(iota((256, H2), 0) < INNER, dw2[0:256, :], 0.0)
    g2[H2 - 8 : H2, :] = g2[H2 - 8 : H2, :] + jnp.where(sub2 >= 5, dw2[248:256, :], 0.0)
    along2 = jnp.sum(v2[0:H2, :] * g2[0:H2, :], axis=0, keepdims=True)
    g2[0:H2, :] = g2[0:H2, :] * scale2 - v2[0:H2, :] * (scale2 * inv2 * inv2 * along2)
    g2[H2 : H2 + 8, :] = dot_nt(jnp.ones((8, LANES), F32), dhead[...], EXACT)
    dbias = jnp.broadcast_to(jnp.sum(sums[1:2, :], axis=1, keepdims=True), (1, LANES))
    pack_first(g1, wide, flat)
    pack_second(g2, flat)
    pack_tail(
        [
            along1 * inv1,
            along2 * inv2,
            jnp.sum(d1, axis=0, keepdims=True),
            jnp.sum(d2, axis=0, keepdims=True),
            dbias,
        ],
        flat,
    )
    gather.finish()
    codes.finish()
    scatter(dims, per_device, kept, flat, buf)
    reduce = Reduce(place, buf, landing, cfg["chunks"], cfg["reduce_orders"], rsend, rrecv, True)
    for k in chunk_ids:
        reduce.start(k, -1)
    for stage in range(-1, 3):
        for k in chunk_ids:
            reduce.arrive(k, stage)
            if stage < 2:
                reduce.start(k, stage + 1)
        spread.arrive(0, stage + 1)
        if stage < 2:
            spread.start(0, stage + 2)
    grad_ref[...] = buf[place.core, place.at[0], place.at[1], place.at[2]]

    everyone = grads_buf[...].reshape(2 * slots, CODE)
    kind = iota((shapes, 2 * slots), 1) & 7
    owner = ((iota((shapes, 2 * slots), 1) >> 3) & (rows - 1)) * 2 + (iota((shapes, 2 * slots), 1) >> int(math.log2(slots)))
    shape_id = iota((shapes, 2 * slots), 0)
    asked = jnp.where(
        kind == 3,
        (shape_id.astype(F32) == shared).astype(F32),
        jnp.where((kind == 4) | (kind == 5), (shape_id == owner * 2 + kind - 4).astype(F32), 0.0),
    )
    code_rows = table_ref.shape[0]
    target_row = dot(codes_of, asked, EXACT)[0:1, :] - 1.0 - base
    pick = (target_row == iota((code_rows, 2 * slots), 0).astype(F32)).astype(F32)
    grad_table = dot(pick, everyone, EXACT)
    here_codes = (codes_of[0:1, :] - 1.0 - base) == iota((code_rows, shapes), 0).astype(F32)
    is_used = jnp.sum(here_codes.astype(F32), axis=1, keepdims=True) > 0.5
    table, code_first, code_second = table_ref[...], code_first_ref[...], code_second_ref[...]
    first_new = BETA_FIRST * code_first + (1.0 - BETA_FIRST) * grad_table
    second_new = BETA_SECOND * code_second + (1.0 - BETA_SECOND) * grad_table * grad_table
    step_vals = (
        CODE_RATE
        * (first_new / (1.0 - BETA_FIRST**STEP))
        / (jnp.sqrt(second_new / (1.0 - BETA_SECOND**STEP)) + ADAM_EPS)
    )
    new_table_ref[...] = jnp.where(is_used, table - step_vals, table)
    new_first_ref[...] = jnp.where(is_used, first_new, code_first)
    new_second_ref[...] = jnp.where(is_used, second_new, code_second)
    loss_ref[...] = jnp.sum(grads_buf[:, :, :, :, 0:8, 0:LANES], axis=(0, 1, 2, 3))[0:1, 0:1]
    spread.finish()
    reduce.finish()


def chunked(rows, count):
    blocks = rows // 8
    count = min(count, blocks)
    out, at = [], 0
    for k in range(count):
        size = (blocks * (k + 1)) // count * 8 - at
        out.append((at, size))
        at += size
    return out


def shards(rows, params, momentum, average, table, code_first, code_second, coords, targets, segment_ids, shape_code):
    per_device = params.shape[0]
    devices = 2 * rows
    used, kept = piece_rows(per_device, devices)
    dims = chip_dims(rows)
    device = lax.axis_index(("rows", "mp"))
    phase = (device * per_device) % LANES
    piece = lax.dynamic_update_slice(jnp.zeros((kept * LANES,), F32), params, (phase,)).reshape(kept, LANES)
    points_here = segment_ids.shape[0]
    tile = 512
    tiles = points_here // tile
    shapes = shape_code.shape[0]
    code_rows = table.shape[0]
    chunks = chunked(kept, 4)
    cfg = dict(
        dims=dims,
        rows=rows,
        per_device=per_device,
        tile=tile,
        shapes=shapes,
        chunks=chunks,
        gather_orders=[(0, 1, 2), (0, 2, 1)],
        reduce_orders=[(1, 2, 0), (2, 1, 0)],
    )
    flat_rows = per_device * devices // LANES + kept + 8
    most = max(dims)
    n = len(chunks)
    vm = pltpu.VMEM
    dma = pltpu.SemaphoreType.DMA
    scratch = [
        vm((2,) + dims + (kept, LANES), F32),
        landings(dims, cfg["reduce_orders"], (kept, LANES)),
        vm((flat_rows, LANES), F32),
        vm((272, 256), F32),
        vm((264, 256), F32),
        vm((520, H2), F32),
        vm((264, 256), F32),
        vm((520, H2), F32),
        vm((H2, 768), BF16),
        vm((256, H2), BF16),
        vm((256, LANES), BF16),
        vm((3, H2, LANES), F32),
        vm((H2, LANES), F32),
        vm((4, tiles, tile), F32),
        vm((784, tile), BF16),
        vm((256, tile), F32),
        vm((256, tile), F32),
        vm((H2, tile), F32),
        vm((H2, tile), F32),
        vm((H2, tile), F32),
        vm((H2, tile), BF16),
        vm((256, tile), F32),
        vm((256, tile), BF16),
        vm((272, H2), F32),
        vm((16, 256), F32),
        vm((H2, LANES), F32),
        vm((8, tile), F32),
        vm((2,) + dims + (8, CODE), F32),
        landings(dims, [(2, 1, 0)], (8, CODE)),
        vm((2,) + dims + (8, CODE), F32),
        dma((n, 4, most)),
        dma((n, 4, most)),
        dma((1, 4, most)),
        dma((1, 4, most)),
        dma((1, 4, most)),
        dma((1, 4, most)),
        dma((n, 4, most)),
        dma((n, 4, most)),
    ]
    spec = pl.BlockSpec(memory_space=pltpu.VMEM)
    loss, grad, new_table, new_first, new_second = pl.pallas_call(
        functools.partial(kernel, cfg),
        out_shape=(
            jax.ShapeDtypeStruct((1, 1), F32),
            jax.ShapeDtypeStruct((kept, LANES), F32),
            jax.ShapeDtypeStruct((code_rows, CODE), F32),
            jax.ShapeDtypeStruct((code_rows, CODE), F32),
            jax.ShapeDtypeStruct((code_rows, CODE), F32),
        ),
        in_specs=[spec] * 8,
        out_specs=(spec,) * 5,
        scratch_shapes=scratch,
        compiler_params=pltpu.CompilerParams(
            collective_id=0, has_side_effects=True, vmem_limit_bytes=56 << 20
        ),
    )(
        piece,
        table,
        code_first,
        code_second,
        coords,
        targets.reshape(-1, LANES),
        segment_ids.reshape(-1, LANES),
        shape_code.reshape(1, shapes),
    )
    grad_shard = lax.dynamic_slice(grad.reshape(-1), (phase,), (per_device,))
    new_momentum = MOMENTUM_DECAY * momentum + grad_shard
    new_params = params - LEARN_RATE * (grad_shard + MOMENTUM_DECAY * new_momentum)
    new_average = AVERAGE_DECAY * average + (1.0 - AVERAGE_DECAY) * new_params
    return (loss.reshape(()), new_momentum, new_params, new_average, new_table, new_first, new_second)


def solution(mesh):
    flat = P(("rows", "mp"))
    placed = (flat, flat, flat, P("rows", None), P("rows", None), P("rows", None), P(None, ("rows", "mp")), flat, flat, P())
    return jax.shard_map(
        functools.partial(shards, mesh.shape["rows"]),
        mesh=mesh,
        in_specs=placed,
        out_specs=(P(), flat, flat, flat, P("rows", None), P("rows", None), P("rows", None)),
        check_vma=False,
    )
```

time: 452 us -> 68.3 us (0.15); the launches traced: 444 us -> 67.9 us
  blocking collectives: 193 us -> 0 us
  waiting for transfers between devices: 102 us -> 0 us
  matrix products: 85 us -> 0 us
  Pallas kernels: 0 us -> 59.7 us
  other arithmetic: 26.2 us -> 1.56 us
  between operations: 20.3 us -> 2.49 us
  local copies, waits for them, and re-layouts: 17.2 us -> 4.15 us
    unnamed x2 -> x0, blocking collectives: 117 us -> none
    unnamed x7 -> x0, waiting for transfers between devices: 102 us -> none
    dot_general x18 -> x0, matrix products: 85 us -> none  [the longest x3 42.6 us: network(): jnp.dot(joined, second_weight, precision=PRECISE) + second_bias]
    pallas_call x0 -> x1, Pallas kernels: none -> 59.7 us  [shards(): pl.pallas_call(functools.partial(kernel, cfg), out_shape=(jax.ShapeDtypeS...]
    all_gather x1 -> x0, blocking collectives: 39.7 us -> none  [shards(): gathered = lax.all_gather(grad_codes, 'rows', axis=0, tiled=True)]
    psum x1 -> x0, blocking collectives: 36.8 us -> none  [shards(): loss_tot, prior_tot = lax.psum((loss_dev, prior_dev), ('rows', 'mp'))]
    reduce_sum x9 -> x0, other arithmetic: 12.6 us -> none  [the longest x1 6.88 us: network(): jnp.dot(joined, second_weight, precision=PRECISE) + second_bias]
    unnamed x51 -> x17, local copies, waits for them, and re-layouts: 9.51 us -> 3.7 us
  transfers between devices with their start and end apart: 4 -> 0, of which waited for: 3 -> 0; matrix products, arithmetic and copies ran while one was open for 5% -> 0% of each run, Pallas kernels for 0% -> 0%
where the time goes in v1:
time: 68.3 us; the launch traced here: 67.9 us
  Pallas kernels  59.7 us (87%)
  local copies, waits for them, and re-layouts  4.15 us (6%)
  between operations  2.49 us (4%)
  other arithmetic  1.56 us (2%)
    pallas_call x1, Pallas kernels, shards(): pl.pallas_call(functools.partial(kernel, cfg), out_shape=(jax.ShapeDtypeS...  59.7 us
    unnamed x17, local copies, waits for them, and re-layouts  3.7 us
    add x1, other arithmetic, shards(): new_average = AVERAGE_DECAY * average + (1.0 - AVERAGE_DECAY) * new_params  1.56 us

profile of v1, /device:TPU:0, one launch (start us, length us, event | category | flops | bytes accessed | tf_op | source)
XLA Modules:
  0.0 67.9 jit_solution(3827194094941960696)
XLA Ops:
  0.6 0.0 copy-start
  0.7 0.8 %copy-done = f32[10304]{0:T(1024)S(1)} copy-done((f32[10304]{0:T(1024)S(1)}, f32[10304]{0:T(1024)}, u32[]{:S(2)}) %copy-start) | copy-done | bytes 41240
  1.4 0.4 dynamic_update_slice.3
  1.9 0.0 copy-start.1
  1.9 0.6 copy-done.1
  2.5 0.0 copy-start.5
  2.5 0.0 copy-start.6
  2.5 59.7 %shard_map.153 = (f32[1,1]{1,0:T(1,128)}, f32[88,128]{1,0:T(8,128)}, f32[64,256]{1,0:T(8,128)}, f32[64,256]{1,0:T(8,128)}, f32[64,256]{1,0:T(8,128)}) custom-call(f32[88,128]{1,0:T(8,128)} %bitcast.6, f32[64,256]{1,0:T(8,128)} %table_ref.1, f32[64,256]{1,0:T(8,128)} %code_first_ref.1, f32[64,256]{1,0:T(8,128)} %code_second_ref.1, f32[3,4096]{1,0:T(4,128)} %coords_ref.1, ...), custom_call_target="tpu_custom_call" | custom-call | tf_op jit(solution)/shard_map/pallas_call | solution.py:797
  62.2 0.0 copy-done.5
  62.2 0.0 copy-done.6
  62.2 0.0 copy-start.4
  62.2 1.6 %multiply_add_fusion = (f32[10304]{0:T(1024)}, f32[10304]{0:T(1024)}, f32[10304]{0:T(1024)}) fusion(f32[10304]{0:T(1024)S(1)} %copy-done.5, f32[10304]{0:T(1024)S(1)} %copy-done, f32[11264]{0:T(1024)} %bitcast.7, s32[]{:T(128)S(6)} %select_n.12, f32[10304]{0:T(1024)S(1)} %copy-done.6), kind=kLoop, calls=%fused_computation | loop fusion | flops 92736 | bytes 288516 | tf_op jit(solution)/shard_map/add | solution.py:825
  64.4 0.0 copy-done.4
  64.4 0.0 copy-start.3
  64.5 0.6 copy.23
  65.1 0.2 copy-done.3
  65.3 0.0 copy-start.2
  65.3 0.6 copy.24
  65.9 0.2 copy-done.2
  66.2 0.6 copy.25
  (1 shorter events, 0.0 us)
Async XLA Ops:
  0.6 0.8 %copy-start = (f32[10304]{0:T(1024)S(1)}, f32[10304]{0:T(1024)}, u32[]{:S(2)}) copy-start(f32[10304]{0:T(1024)} %param.10) | copy-start | bytes 123652
  1.9 0.6 copy-start.1
  2.5 59.7 %copy-start.5 = (f32[10304]{0:T(1024)S(1)}, f32[10304]{0:T(1024)}, u32[]{:S(2)}) copy-start(f32[10304]{0:T(1024)} %param.12) | copy-start | bytes 123652
  2.5 59.7 %copy-start.6 = (f32[10304]{0:T(1024)S(1)}, f32[10304]{0:T(1024)}, u32[]{:S(2)}) copy-start(f32[10304]{0:T(1024)} %param.11) | copy-start | bytes 123652
  62.2 2.2 %copy-start.4 = (f32[64,256]{1,0:T(8,128)S(1)}, f32[64,256]{1,0:T(8,128)}, u32[]{:S(2)}) copy-start(f32[64,256]{1,0:T(8,128)} %get-tuple-element.31) | copy-start | bytes 196612
  64.4 0.8 %copy-start.3 = (f32[64,256]{1,0:T(8,128)S(1)}, f32[64,256]{1,0:T(8,128)}, u32[]{:S(2)}) copy-start(f32[64,256]{1,0:T(8,128)} %get-tuple-element.32) | copy-start | bytes 196612
  65.3 0.9 %copy-start.2 = (f32[64,256]{1,0:T(8,128)S(1)}, f32[64,256]{1,0:T(8,128)}, u32[]{:S(2)}) copy-start(f32[64,256]{1,0:T(8,128)} %get-tuple-element.33) | copy-start | bytes 196612

commit v2 on v1

--- a/solution.py
+++ b/solution.py
@@ -221,6 +221,67 @@
     return jnp.concatenate([x[k : k + 1] for k in range(count)], axis=1)
 
 
+def rows_of(ref, count):
+    whole = count // LANES
+    rows = ref[pl.ds(0, whole * LANES)].reshape(whole, LANES)
+    if count % LANES:
+        rest = ref[pl.ds(whole * LANES, count % LANES)].reshape(1, count % LANES)
+        rows = jnp.concatenate([rows, widen(rest, LANES)], axis=0)
+    return rows
+
+
+def store_rows(ref, rows, count):
+    whole = count // LANES
+    ref[pl.ds(0, whole * LANES)] = rows[:whole].reshape(whole * LANES)
+    if count % LANES:
+        ref[pl.ds(whole * LANES, count % LANES)] = rows[whole : whole + 1, : count % LANES].reshape(count % LANES)
+
+
+def update(
+    per_device,
+    grad_ref,
+    grad_table_ref,
+    used_ref,
+    loss_in_ref,
+    params_ref,
+    momentum_ref,
+    average_ref,
+    table_ref,
+    code_first_ref,
+    code_second_ref,
+    loss_ref,
+    new_momentum_ref,
+    new_params_ref,
+    new_average_ref,
+    new_table_ref,
+    new_first_ref,
+    new_second_ref,
+):
+    count = -(-per_device // LANES)
+    grad = grad_ref[0:count, :]
+    params = rows_of(params_ref, per_device)
+    new_momentum = MOMENTUM_DECAY * rows_of(momentum_ref, per_device) + grad
+    new_params = params - LEARN_RATE * (grad + MOMENTUM_DECAY * new_momentum)
+    new_average = AVERAGE_DECAY * rows_of(average_ref, per_device) + (1.0 - AVERAGE_DECAY) * new_params
+    store_rows(new_momentum_ref, new_momentum, per_device)
+    store_rows(new_params_ref, new_params, per_device)
+    store_rows(new_average_ref, new_average, per_device)
+    grad_table = grad_table_ref[...]
+    is_used = used_ref[...] > 0.5
+    table, code_first, code_second = table_ref[...], code_first_ref[...], code_second_ref[...]
+    first_new = BETA_FIRST * code_first + (1.0 - BETA_FIRST) * grad_table
+    second_new = BETA_SECOND * code_second + (1.0 - BETA_SECOND) * grad_table * grad_table
+    step_vals = (
+        CODE_RATE
+        * (first_new / (1.0 - BETA_FIRST**STEP))
+        / (jnp.sqrt(second_new / (1.0 - BETA_SECOND**STEP)) + ADAM_EPS)
+    )
+    new_table_ref[...] = jnp.where(is_used, table - step_vals, table)
+    new_first_ref[...] = jnp.where(is_used, first_new, code_first)
+    new_second_ref[...] = jnp.where(is_used, second_new, code_second)
+    loss_ref[...] = loss_in_ref[...]
+
+
 def bounds(devices, per_device):
     for d in range(devices):
         row, phase = divmod(per_device * d, LANES)
@@ -363,19 +424,16 @@
 
 def kernel(
     cfg,
-    piece_ref,
+    params_ref,
     table_ref,
-    code_first_ref,
-    code_second_ref,
     coords_ref,
     targets_ref,
     seg_ref,
     shape_code_ref,
     loss_ref,
     grad_ref,
-    new_table_ref,
-    new_first_ref,
-    new_second_ref,
+    grad_table_ref,
+    used_ref,
     buf,
     landing,
     flat,
@@ -396,6 +454,7 @@
     h2,
     act,
     second,
+    preds,
     d2b,
     df,
     d1b,
@@ -432,7 +491,6 @@
         for o in place.steps(dim):
             pl.semaphore_signal(barrier, inc=1, device_id=place.peer(dim, o)[1], device_id_type=MESH)
             greeted += 1
-    pl.semaphore_wait(barrier, greeted)
 
     seg_heads = seg_ref[0 : head_len // LANES, :].astype(F32)
     shared = jnp.max(jnp.max(seg_heads, axis=1, keepdims=True), axis=0, keepdims=True)
@@ -448,16 +506,17 @@
     mine = (device * 2).astype(F32)
     counts = [count(seg == shared), count(seg == mine), count(seg == mine + 1.0)]
 
+    phase = (device * per_device) % LANES
     own = buf.at[place.core, place.at[0], place.at[1], place.at[2]]
-    own[0 : kept - 8, :] = piece_ref[0 : kept - 8, :]
-    own[kept - 8 : kept, :] = jnp.where(
-        iota((8, LANES), 0) == 7, jnp.broadcast_to(counts[0], (8, LANES)), piece_ref[kept - 8 : kept, :]
-    )
-
-    gather = Gather(place, buf, cfg["chunks"], cfg["gather_orders"], psend, precv)
-    chunk_ids = range(len(cfg["chunks"]))
-    for k in chunk_ids:
-        gather.start(k, 0)
+    raw = rows_of(params_ref, per_device)
+    raw = jnp.concatenate(
+        [raw, jnp.zeros((kept - 1 - raw.shape[0], LANES), F32), jnp.broadcast_to(counts[0], (1, LANES))], axis=0
+    )
+    if any(p for _, _, p, _ in bounds(2 * rows, per_device)):
+        moved = pltpu.roll(raw, phase, 1)
+        before = jnp.concatenate([jnp.zeros((1, LANES), F32), moved[: kept - 1]], axis=0)
+        raw = jnp.where((iota((kept, LANES), 1) < phase) & (iota((kept, LANES), 0) < kept - 1), before, moved)
+    own[...] = raw
 
     base = (place.row * table_ref.shape[0]).astype(F32)
     codes_of = jnp.broadcast_to(shape_code_ref[...].astype(F32) + 1.0, (8, shapes))
@@ -474,6 +533,13 @@
     pick = (wanted == iota((slots, table_ref.shape[0]), 1).astype(F32)).astype(F32)
     answer = dot(pick, table_ref[...], EXACT)
     codes_buf[place.core] = answer.reshape(dims + (8, CODE))
+
+    pl.semaphore_wait(barrier, greeted)
+    gather = Gather(place, buf, cfg["chunks"], cfg["gather_orders"], psend, precv)
+    chunk_ids = range(len(cfg["chunks"]))
+    for k in chunk_ids:
+        gather.start(k, 0)
+
     codes = Reduce(place, codes_buf, codes_landing, [(0, 8)], [(2, 1, 0)], csend, crecv, False)
     codes.start(0, 0)
 
@@ -531,8 +597,7 @@
     for k in range(3):
         bias[k] = jnp.broadcast_to(columns[:, 3 + k : 4 + k], (H2, LANES))
     head[...] = jnp.broadcast_to(columns[:, 6:7], (H2, LANES))
-    xyz2 = pltpu.roll(v2[H2 - 8 : H2, :], 0, 0)
-    last = jnp.where(iota((8, H2), 0) < 5, v2[248:256, :], xyz2)
+    last = jnp.where(sub2 < 5, v2[248:256, :], v2[H2 - 8 : H2, :])
     normal = jnp.concatenate([v2[0:248, :], last], axis=0) * scale2
     w2b[...] = normal.astype(BF16)
     high, low = split2(0.5 * normal.T)
@@ -546,63 +611,69 @@
     sums[...] = jnp.zeros(sums.shape, F32)
     block = 32
 
-    def one_tile(t, _):
-        at = pl.ds(pl.multiple_of(t * tile, tile), tile)
-        two = points[3, pl.ds(t, 1), :]
-        here = t * tile + iota((1, tile), 1)
-        is_head = (here < head_len).astype(F32)
-        one = 1.0 - two - is_head
+    def lanes_of(q):
+        return slice(q * LANES, (q + 1) * LANES)
+
+    def first_layer(t):
+        at = slice(t * tile, (t + 1) * tile)
+        two = points[3, t : t + 1, :]
+        is_head = (t * tile + iota((1, tile), 1) < head_len).astype(F32)
         x8 = jnp.concatenate(
-            [coords_ref[:, at], is_head, one, two, jnp.zeros((2, tile), F32)], axis=0
+            [coords_ref[:, at], is_head, 1.0 - two - is_head, two, jnp.zeros((2, tile), F32)], axis=0
         )
         xa, xb, xc = split3(x8)
         x48 = jnp.concatenate([xa, xb, xa, xb, xc, xa], axis=0).astype(BF16)
-        hc[768:784, :] = jnp.concatenate([xa, xb], axis=0).astype(BF16)
+        hc[t % 2, 768:784, :] = jnp.concatenate([xa, xb], axis=0).astype(BF16)
         h1[...] = dot(w0[:, 0:48], x48)
-        for u in range(0, 256, block):
-            for q in range(per_tile):
-                lanes = slice(q * LANES, (q + 1) * LANES)
+        for q in range(per_tile):
+            lanes = lanes_of(q)
+            for u in range(0, 256, block):
                 us = slice(u, u + block)
                 h = h1[us, lanes]
                 th = jnp.tanh(h)
                 m = h * th
                 f = h + m
-                slope1[us, lanes] = (0.5 + 0.5 * th) * (1.0 + (h - m))
+                slope1[t % 2, us, lanes] = (0.5 + 0.5 * th) * (1.0 + (h - m))
                 if u + block > INNER:
                     f = jnp.where(iota((block, LANES), 0) + u >= INNER, h, f)
                 fh, fl = split2(f)
-                hc[us, lanes] = fh
-                hc[256 + u : 256 + u + block, lanes] = fl
-                hc[512 + u : 512 + u + block, lanes] = fh
-        h2[...] = dot(w2t[...], hc[0:768, :])
+                hc[t % 2, us, lanes] = fh
+                hc[t % 2, 256 + u : 256 + u + block, lanes] = fl
+                hc[t % 2, 512 + u : 512 + u + block, lanes] = fh
+
+    def second_product(t):
+        h2[t % 2] = dot(w2t[...], hc[t % 2, 0:768, :])
+
+    def second_layer(t):
         parts = []
         for q in range(per_tile):
-            lanes = slice(q * LANES, (q + 1) * LANES)
+            lanes = lanes_of(q)
             in_head = t * per_tile + q < head_len // LANES
-            b_one = jnp.where(in_head, 0, 1)
-            b_two = jnp.where(in_head, 0, 2)
-            is_second = jnp.broadcast_to(two[:, lanes], (block, LANES)) > 0.5
+            is_second = jnp.broadcast_to(points[3, t : t + 1, lanes], (block, LANES)) > 0.5
             part = jnp.zeros((8, LANES), F32)
             for u in range(0, H2, block):
                 us = slice(u, u + block)
-                h = h2[us, lanes] + jnp.where(is_second, bias[b_two, us, :], bias[b_one, us, :])
+                b = bias[0, us, :] if in_head else jnp.where(is_second, bias[2, us, :], bias[1, us, :])
+                h = h2[t % 2, us, lanes] + b
                 th = jnp.tanh(h)
                 m = h * th
                 s = h + m
                 hw = head[us, :]
-                second[us, lanes] = s
-                act[us, lanes] = hw * ((1.0 + th) * (1.0 + (h - m)))
+                second[t % 2, us, lanes] = s
+                act[t % 2, us, lanes] = hw * ((1.0 + th) * (1.0 + (h - m)))
                 w = hw * s
                 for v in range(0, block, 8):
                     part = part + w[v : v + 8]
             parts.append(jnp.sum(part, axis=0, keepdims=True))
-        raw = 2.0 * jnp.concatenate(parts, axis=1) + hbias
-        pred = jnp.tanh(raw)
+        preds[t % 2, 0:1, :] = 2.0 * jnp.concatenate(parts, axis=1) + hbias
+
+    def back_second(t):
+        pred = jnp.tanh(preds[t % 2, 0:1, :])
         squash = jnp.tanh(pred * (1.0 / CLAMP_DELTA))
-        resid = CLAMP_DELTA * squash - CLAMP_DELTA * points[1, pl.ds(t, 1), :]
+        resid = CLAMP_DELTA * squash - CLAMP_DELTA * points[1, t : t + 1, :]
         square = resid * resid + SMOOTH * SMOOTH
         inv_radius = lax.rsqrt(square)
-        share = points[2, pl.ds(t, 1), :]
+        share = points[2, t : t + 1, :]
         dpred = share * (resid * inv_radius) * (1.0 - squash * squash) * (1.0 - pred * pred)
         sums[0:1, :] = sums[0:1, :] + share * (square * inv_radius - SMOOTH)
         sums[1:2, :] = sums[1:2, :] + dpred
@@ -610,20 +681,35 @@
             us = slice(u, u + block)
             total_u = dhead[us, :]
             for q in range(per_tile):
-                lanes = slice(q * LANES, (q + 1) * LANES)
+                lanes = lanes_of(q)
                 dp = jnp.broadcast_to(dpred[:, lanes], (block, LANES))
-                d2b[us, lanes] = (act[us, lanes] * dp).astype(BF16)
-                total_u = total_u + second[us, lanes] * dp
+                d2b[t % 2, us, lanes] = (act[t % 2, us, lanes] * dp).astype(BF16)
+                total_u = total_u + second[t % 2, us, lanes] * dp
             dhead[us, :] = total_u
-        df[...] = dot(w2b[...], d2b[...])
-        dw2[...] = dw2[...] + dot_nt(hc[512:784, :], d2b[...])
+
+    def back_products(t):
+        df[...] = dot(w2b[...], d2b[t % 2])
+        dw2[...] = dw2[...] + dot_nt(hc[t % 2, 512:784, :], d2b[t % 2])
+
+    def back_first(t):
         for u in range(0, 256, block):
             us = slice(u, u + block)
-            d1b[us, :] = (df[us, :] * slope1[us, :]).astype(BF16)
-        dw1[...] = dw1[...] + dot_nt(hc[768:784, :], d1b[...])
-        return 0
-
-    lax.fori_loop(0, tiles, one_tile, 0)
+            d1b[us, :] = (df[us, :] * slope1[t % 2, us, :]).astype(BF16)
+        dw1[...] = dw1[...] + dot_nt(hc[t % 2, 768:784, :], d1b[...])
+
+    first_layer(0)
+    for t in range(tiles + 1):
+        if t < tiles:
+            second_product(t)
+        if t > 0:
+            back_second(t - 1)
+            back_products(t - 1)
+        if t < tiles:
+            second_layer(t)
+        if t > 0:
+            back_first(t - 1)
+        if t + 1 < tiles:
+            first_layer(t + 1)
 
     outer1 = jnp.where(lane1 < INNER, dw1[0:8, :] + dw1[8:16, :], 0.0)
     outer2 = dw2[256:264, :] + dw2[264:272, :]
@@ -680,7 +766,12 @@
         spread.arrive(0, stage + 1)
         if stage < 2:
             spread.start(0, stage + 2)
-    grad_ref[...] = buf[place.core, place.at[0], place.at[1], place.at[2]]
+    piece = own[...]
+    if any(p for _, _, p, _ in bounds(2 * rows, per_device)):
+        moved = pltpu.roll(piece, (LANES - phase) % LANES, 1)
+        after = jnp.concatenate([moved[1:], moved[:1]], axis=0)
+        piece = jnp.where(iota((kept, LANES), 1) < LANES - phase, moved, after)
+    grad_ref[...] = piece
 
     everyone = grads_buf[...].reshape(2 * slots, CODE)
     kind = iota((shapes, 2 * slots), 1) & 7
@@ -697,17 +788,8 @@
     grad_table = dot(pick, everyone, EXACT)
     here_codes = (codes_of[0:1, :] - 1.0 - base) == iota((code_rows, shapes), 0).astype(F32)
     is_used = jnp.sum(here_codes.astype(F32), axis=1, keepdims=True) > 0.5
-    table, code_first, code_second = table_ref[...], code_first_ref[...], code_second_ref[...]
-    first_new = BETA_FIRST * code_first + (1.0 - BETA_FIRST) * grad_table
-    second_new = BETA_SECOND * code_second + (1.0 - BETA_SECOND) * grad_table * grad_table
-    step_vals = (
-        CODE_RATE
-        * (first_new / (1.0 - BETA_FIRST**STEP))
-        / (jnp.sqrt(second_new / (1.0 - BETA_SECOND**STEP)) + ADAM_EPS)
-    )
-    new_table_ref[...] = jnp.where(is_used, table - step_vals, table)
-    new_first_ref[...] = jnp.where(is_used, first_new, code_first)
-    new_second_ref[...] = jnp.where(is_used, second_new, code_second)
+    grad_table_ref[...] = grad_table
+    used_ref[...] = jnp.broadcast_to(is_used.astype(F32), used_ref.shape)
     loss_ref[...] = jnp.sum(grads_buf[:, :, :, :, 0:8, 0:LANES], axis=(0, 1, 2, 3))[0:1, 0:1]
     spread.finish()
     reduce.finish()
@@ -729,11 +811,8 @@
     devices = 2 * rows
     used, kept = piece_rows(per_device, devices)
     dims = chip_dims(rows)
-    device = lax.axis_index(("rows", "mp"))
-    phase = (device * per_device) % LANES
-    piece = lax.dynamic_update_slice(jnp.zeros((kept * LANES,), F32), params, (phase,)).reshape(kept, LANES)
     points_here = segment_ids.shape[0]
-    tile = 512
+    tile = 1024
     tiles = points_here // tile
     shapes = shape_code.shape[0]
     code_rows = table.shape[0]
@@ -768,13 +847,14 @@
         vm((3, H2, LANES), F32),
         vm((H2, LANES), F32),
         vm((4, tiles, tile), F32),
-        vm((784, tile), BF16),
+        vm((2, 784, tile), BF16),
         vm((256, tile), F32),
-        vm((256, tile), F32),
-        vm((H2, tile), F32),
-        vm((H2, tile), F32),
-        vm((H2, tile), F32),
-        vm((H2, tile), BF16),
+        vm((2, 256, tile), F32),
+        vm((2, H2, tile), F32),
+        vm((2, H2, tile), F32),
+        vm((2, H2, tile), F32),
+        vm((2, 8, tile), F32),
+        vm((2, H2, tile), BF16),
         vm((256, tile), F32),
         vm((256, tile), BF16),
         vm((272, H2), F32),
@@ -794,36 +874,37 @@
         dma((n, 4, most)),
     ]
     spec = pl.BlockSpec(memory_space=pltpu.VMEM)
-    loss, grad, new_table, new_first, new_second = pl.pallas_call(
+    loss, grad, grad_table, marks = pl.pallas_call(
         functools.partial(kernel, cfg),
         out_shape=(
             jax.ShapeDtypeStruct((1, 1), F32),
             jax.ShapeDtypeStruct((kept, LANES), F32),
             jax.ShapeDtypeStruct((code_rows, CODE), F32),
             jax.ShapeDtypeStruct((code_rows, CODE), F32),
-            jax.ShapeDtypeStruct((code_rows, CODE), F32),
         ),
-        in_specs=[spec] * 8,
-        out_specs=(spec,) * 5,
+        in_specs=[spec] * 6,
+        out_specs=(spec,) * 4,
         scratch_shapes=scratch,
         compiler_params=pltpu.CompilerParams(
             collective_id=0, has_side_effects=True, vmem_limit_bytes=56 << 20
         ),
     )(
-        piece,
+        params,
         table,
-        code_first,
-        code_second,
         coords,
         targets.reshape(-1, LANES),
         segment_ids.reshape(-1, LANES),
         shape_code.reshape(1, shapes),
     )
-    grad_shard = lax.dynamic_slice(grad.reshape(-1), (phase,), (per_device,))
-    new_momentum = MOMENTUM_DECAY * momentum + grad_shard
-    new_params = params - LEARN_RATE * (grad_shard + MOMENTUM_DECAY * new_momentum)
-    new_average = AVERAGE_DECAY * average + (1.0 - AVERAGE_DECAY) * new_params
-    return (loss.reshape(()), new_momentum, new_params, new_average, new_table, new_first, new_second)
+    flat_out = jax.ShapeDtypeStruct((per_device,), F32)
+    table_out = jax.ShapeDtypeStruct((code_rows, CODE), F32)
+    outs = pl.pallas_call(
+        functools.partial(update, per_device),
+        out_shape=(jax.ShapeDtypeStruct((1, 1), F32),) + (flat_out,) * 3 + (table_out,) * 3,
+        in_specs=[spec] * 10,
+        out_specs=(spec,) * 7,
+    )(grad, grad_table, marks, loss, params, momentum, average, table, code_first, code_second)
+    return (outs[0].reshape(()),) + tuple(outs[1:])
 
 
 def solution(mesh):

time: 68.3 us -> 57.3 us (0.84)
  local copies, waits for them, and re-layouts: 4.15 us -> 0 us
  Pallas kernels: 59.7 us -> 56.5 us
  between operations: 2.49 us -> 0.64 us
  other arithmetic: 1.56 us -> 0 us
    pallas_call x1, Pallas kernels: 59.7 us -> 54 us  [shards(): pl.pallas_call(functools.partial(kernel, cfg), out_shape=(jax.ShapeDtypeS...]
    unnamed x17 -> x0, local copies, waits for them, and re-layouts: 3.7 us -> none
    pallas_call x0 -> x1, Pallas kernels: none -> 2.44 us  [shards(): pl.pallas_call(functools.partial(update, per_device), out_shape=(jax.Shap...]
    add x1 -> x0, other arithmetic: 1.56 us -> none  [shards(): new_average = AVERAGE_DECAY * average + (1.0 - AVERAGE_DECAY) * new_params]
where the time goes in v2:
time: 57.3 us; the launch traced here: 57.1 us
  Pallas kernels  56.5 us (99%)
  between operations  0.64 us (1%)
    pallas_call x1, Pallas kernels, shards(): pl.pallas_call(functools.partial(kernel, cfg), out_shape=(jax.ShapeDtypeS...  54 us
    pallas_call x1, Pallas kernels, shards(): pl.pallas_call(functools.partial(update, per_device), out_shape=(jax.Shap...  2.44 us

profile of v2, /device:TPU:0, one launch (start us, length us, event | category | flops | bytes accessed | tf_op | source)
XLA Modules:
  0.0 57.1 jit_solution(9024013469638688390)
XLA Ops:
  0.6 54.0 %shard_map.153 = (f32[1,1]{1,0:T(1,128)}, f32[88,128]{1,0:T(8,128)}, f32[64,256]{1,0:T(8,128)}, f32[64,256]{1,0:T(8,128)}) custom-call(f32[10304]{0:T(1024)} %params_ref.3, f32[64,256]{1,0:T(8,128)} %table_ref.3, f32[3,4096]{1,0:T(4,128)} %coords_ref.1, f32[32,128]{1,0:T(8,128)} %bitcast.4, s32[32,128]{1,0:T(8,128)} %bitcast.5, s32[1,64]{1,0:T(1,128)} %bitcast.6), custom_call_target="tpu_custom_call" | custom-call | tf_op jit(solution)/shard_map/pallas_call | solution.py:877
  54.7 2.4 %shard_map.154 = (f32[1,1]{1,0:T(1,128)}, f32[10304]{0:T(1024)}, f32[10304]{0:T(1024)}, f32[10304]{0:T(1024)}, f32[64,256]{1,0:T(8,128)}, /*index=5*/f32[64,256]{1,0:T(8,128)}, f32[64,256]{1,0:T(8,128)}) custom-call(f32[88,128]{1,0:T(8,128)} %get-tuple-element.18.grad_ref, f32[64,256]{1,0:T(8,128)} %get-tuple-element.19.grad_table_ref, ...), custom_call_target="tpu_custom_call" | custom-call | tf_op jit(solution)/shard_map/pallas_call | solution.py:901

commit v3 on v2

--- a/solution.py
+++ b/solution.py
@@ -1,4 +1,5 @@
 import functools
+import itertools
 import math
 
 import jax
@@ -11,6 +12,8 @@
 MESH = pl.DeviceIdType.MESH
 F32, BF16 = jnp.float32, jnp.bfloat16
 EXACT = lax.Precision.HIGHEST
+THREE = lax.Precision.HIGH
+DEEP = 8
 CODE = 256
 H2 = 512
 INNER = H2 - CODE - 3
@@ -42,7 +45,7 @@
 def piece_rows(per_device, devices):
     most = max((per_device * d) % LANES for d in range(devices))
     rows = -(-(most + per_device) // LANES)
-    return rows, (rows // 8 + 1) * 8
+    return rows, rows + 1
 
 
 class Place:
@@ -53,17 +56,23 @@
         d0, d1, d2 = dims
         self.at = [self.row // (d1 * d2), (self.row // d2) % d1, self.row % d2]
 
-    def peer(self, dim, step):
-        at = list(self.at)
-        at[dim] = (at[dim] + step) % self.dims[dim]
+    def peer(self, steps):
         d0, d1, d2 = self.dims
-        return at[dim], ((at[0] * d1 + at[1]) * d2 + at[2], self.core)
+        at = [(a + o) % d if o else a for a, o, d in zip(self.at, steps, self.dims)]
+        return at, ((at[0] * d1 + at[1]) * d2 + at[2], self.core)
 
     def sibling(self):
         return (self.row, 1 - self.core)
 
-    def steps(self, dim):
-        return range(1, self.dims[dim])
+
+def steps_of(dims, stage):
+    ranges = [range(dims[d]) if d in stage else range(1) for d in range(3)]
+    return [o for o in itertools.product(*ranges) if any(o)]
+
+
+def rest_of(dims, order, stage):
+    gone = [d for axes in order[: stage + 1] for d in axes]
+    return tuple(dims[d] for d in range(3) if d not in gone)
 
 
 def remote(src, dst, send, recv, device):
@@ -73,34 +82,38 @@
 
 
 class Gather:
-    def __init__(self, place, buf, chunks, orders, send, recv):
-        self.p, self.buf, self.chunks, self.orders = place, buf, chunks, orders
+    def __init__(self, place, buf, chunks, send, recv):
+        self.p, self.buf, self.chunks = place, buf, chunks
         self.send, self.recv, self.live = send, recv, {}
 
-    def view(self, done, core, k):
-        idx = [slice(None) if d in done else self.p.at[d] for d in range(3)]
-        begin, size = self.chunks[k]
-        return self.buf.at[core, idx[0], idx[1], idx[2], pl.ds(begin, size)]
-
     def start(self, k, stage):
-        order = self.orders[k % len(self.orders)]
-        core = self.p.core
-        copies = []
-        if stage == 3:
-            v = self.view(order, core, k)
-            copies.append(remote(v, v, self.send.at[k, 3, 0], self.recv.at[k, 3, 0], self.p.sibling()))
+        begin, size, order = self.chunks[k]
+        done = [d for axes in order[:stage] for d in axes]
+        idx = tuple(slice(None) if d in done else self.p.at[d] for d in range(3))
+        v = self.buf.at[(self.p.core,) + idx + (pl.ds(begin, size),)]
+        if stage == len(order):
+            devices = [self.p.sibling()]
         else:
-            for o in self.p.steps(order[stage]):
-                v = self.view(order[:stage], core, k)
-                dev = self.p.peer(order[stage], o)[1]
-                copies.append(remote(v, v, self.send.at[k, stage, o], self.recv.at[k, stage, o], dev))
-        for c in copies:
+            devices = [self.p.peer(o)[1] for o in steps_of(self.p.dims, order[stage])]
+        self.live[k, stage] = [
+            remote(v, v, self.send.at[k, stage, i], self.recv.at[k, stage, i], device)
+            for i, device in enumerate(devices)
+        ]
+        for c in self.live[k, stage]:
             c.start()
-        self.live[k, stage] = copies
 
     def arrive(self, k, stage):
         for c in self.live[k, stage]:
             c.wait_recv()
+
+    def run(self):
+        for stage in range(max(len(order) for _, _, order in self.chunks) + 1):
+            for k, (_, _, order) in enumerate(self.chunks):
+                if stage <= len(order):
+                    self.arrive(k, stage)
+                    if stage < len(order):
+                        self.start(k, stage + 1)
+            yield
 
     def finish(self):
         for copies in self.live.values():
@@ -109,69 +122,64 @@
 
 
 class Reduce:
-    def __init__(self, place, buf, landing, chunks, orders, send, recv, cores):
-        self.p, self.buf, self.landing, self.chunks, self.orders = place, buf, landing, chunks, orders
-        self.send, self.recv, self.cores, self.live = send, recv, cores, {}
-
-    def index(self, k, stage, last):
-        order = self.orders[k % len(self.orders)]
-        idx = [self.p.at[d] if d in order[:stage] else slice(None) for d in range(3)]
-        if last is not None:
-            idx[order[stage]] = last
-        begin, size = self.chunks[k]
-        return tuple(idx) + (pl.ds(begin, size),)
-
-    def landed(self, k, stage, o):
-        ref = self.landing[1 + 3 * (k % len(self.orders)) + stage]
-        begin, size = self.chunks[k]
-        return ref.at[(o - 1,) + (slice(None),) * (2 - stage) + (pl.ds(begin, size),)]
+    def __init__(self, place, buf, landing, chunks, send, recv, cores):
+        self.p, self.buf, self.landing, self.chunks = place, buf, landing, chunks
+        self.send, self.recv, self.first, self.live = send, recv, -1 if cores else 0, {}
+
+    def index(self, k, stage, at):
+        begin, size, order = self.chunks[k]
+        gone = [d for axes in order[: stage + 1] for d in axes]
+        return tuple(at[d] if d in gone else slice(None) for d in range(3)) + (pl.ds(begin, size),)
+
+    def landed(self, k, stage, i):
+        begin, size, order = self.chunks[k]
+        rest = len(rest_of(self.p.dims, order, stage))
+        return self.landing[k][stage + 1].at[(i,) + (slice(None),) * (rest + 2)]
 
     def start(self, k, stage):
-        order = self.orders[k % len(self.orders)]
+        order = self.chunks[k][2]
         copies = []
         if stage < 0:
-            idx = self.index(k, 0, None)
-            copies.append(
-                remote(
-                    self.buf.at[(1 - self.p.core,) + idx],
-                    self.landing[0].at[idx],
-                    self.send.at[k, 3, 0],
-                    self.recv.at[k, 3, 0],
-                    self.p.sibling(),
-                )
+            src = self.buf.at[(1 - self.p.core,) + self.index(k, -1, None)]
+            copies.append((src, self.p.sibling()))
+        else:
+            for o in steps_of(self.p.dims, order[stage]):
+                at, device = self.p.peer(o)
+                copies.append((self.buf.at[(self.p.core,) + self.index(k, stage, at)], device))
+        self.live[k, stage] = [
+            remote(
+                src,
+                self.landed(k, stage, i),
+                self.send.at[k, stage + 1, i],
+                self.recv.at[k, stage + 1, i],
+                device,
             )
-        else:
-            for o in self.p.steps(order[stage]):
-                at, dev = self.p.peer(order[stage], o)
-                idx = self.index(k, stage, at)
-                copies.append(
-                    remote(
-                        self.buf.at[(self.p.core,) + idx],
-                        self.landed(k, stage, o),
-                        self.send.at[k, stage, o],
-                        self.recv.at[k, stage, o],
-                        dev,
-                    )
-                )
-        for c in copies:
+            for i, (src, device) in enumerate(copies)
+        ]
+        for c in self.live[k, stage]:
             c.start()
-        self.live[k, stage] = copies
 
     def arrive(self, k, stage):
+        mine = (self.p.core,) + self.index(k, stage, self.p.at)
         for c in self.live[k, stage]:
             c.wait_recv()
-        order = self.orders[k % len(self.orders)]
-        if stage < 0:
-            idx = self.index(k, 0, None)
-            mine = (self.p.core,) + idx
-            self.buf[mine] = self.buf[mine] + self.landing[0][idx]
-        else:
-            idx = self.index(k, stage, self.p.at[order[stage]])
-            mine = (self.p.core,) + idx
-            total = self.buf[mine]
-            for o in self.p.steps(order[stage]):
-                total = total + self.landed(k, stage, o)[...]
-            self.buf[mine] = total
+        total = self.buf[mine]
+        for i in range(len(self.live[k, stage])):
+            total = total + self.landed(k, stage, i)[...]
+        self.buf[mine] = total
+
+    def begin(self):
+        for k in range(len(self.chunks)):
+            self.start(k, self.first)
+
+    def run(self):
+        for stage in range(self.first, max(len(order) for _, _, order in self.chunks)):
+            for k, (_, _, order) in enumerate(self.chunks):
+                if stage < len(order):
+                    self.arrive(k, stage)
+                    if stage + 1 < len(order):
+                        self.start(k, stage + 1)
+            yield
 
     def finish(self):
         for copies in self.live.values():
@@ -179,13 +187,20 @@
                 c.wait_send()
 
 
-def landings(dims, orders, tail):
-    shapes = [tuple(dims) + tail]
-    for order in orders:
-        for stage, d in enumerate(order):
-            rest = tuple(dims[e] for e in range(3) if e not in order[: stage + 1])
-            shapes.append((max(dims[d] - 1, 1),) + rest + tail)
-    return [pltpu.VMEM(shape, F32) for shape in shapes]
+def landings(dims, chunks, width, cores):
+    out = []
+    for _, size, order in chunks:
+        shapes = [(1,) + tuple(dims) + (size, width) if cores else (1, 8, 128)]
+        for stage, axes in enumerate(order):
+            shapes.append((len(steps_of(dims, axes)),) + rest_of(dims, order, stage) + (size, width))
+        out.append([pltpu.VMEM(tuple(max(n, 1) for n in shape), F32) for shape in shapes])
+    return out
+
+
+def semaphores(dims, chunks):
+    stages = max(len(order) for _, _, order in chunks) + 1
+    most = max(len(steps_of(dims, axes)) for _, _, order in chunks for axes in order)
+    return [pltpu.SemaphoreType.DMA((len(chunks), stages, max(most, 1)))] * 2
 
 
 def iota(shape, dim):
@@ -241,7 +256,7 @@
     per_device,
     grad_ref,
     grad_table_ref,
-    used_ref,
+    shape_code_ref,
     loss_in_ref,
     params_ref,
     momentum_ref,
@@ -267,7 +282,9 @@
     store_rows(new_params_ref, new_params, per_device)
     store_rows(new_average_ref, new_average, per_device)
     grad_table = grad_table_ref[...]
-    is_used = used_ref[...] > 0.5
+    code_rows = table_ref.shape[0]
+    here = shape_code_ref[...] - lax.axis_index("rows") * code_rows == iota((code_rows, shape_code_ref.shape[1]), 0)
+    is_used = jnp.sum(here.astype(F32), axis=1, keepdims=True) > 0.5
     table, code_first, code_second = table_ref[...], code_first_ref[...], code_second_ref[...]
     first_new = BETA_FIRST * code_first + (1.0 - BETA_FIRST) * grad_table
     second_new = BETA_SECOND * code_second + (1.0 - BETA_SECOND) * grad_table * grad_table
@@ -424,16 +441,22 @@
 
 def kernel(
     cfg,
+    params_hbm,
+    table_hbm,
+    coords_hbm,
+    targets_hbm,
+    seg_hbm,
+    shape_code_hbm,
+    loss_ref,
+    grad_ref,
+    grad_table_ref,
     params_ref,
     table_ref,
     coords_ref,
     targets_ref,
     seg_ref,
     shape_code_ref,
-    loss_ref,
-    grad_ref,
-    grad_table_ref,
-    used_ref,
+    fetched,
     buf,
     landing,
     flat,
@@ -485,38 +508,56 @@
     head_len = seg_ref.shape[0] * LANES // 16
 
     barrier = pltpu.get_barrier_semaphore()
-    greeted = 1
+    greeted = {place_steps for table in cfg["tables"] for _, _, order in table for axes in order for place_steps in steps_of(dims, axes)}
     pl.semaphore_signal(barrier, inc=1, device_id=place.sibling(), device_id_type=MESH)
-    for dim in range(3):
-        for o in place.steps(dim):
-            pl.semaphore_signal(barrier, inc=1, device_id=place.peer(dim, o)[1], device_id_type=MESH)
-            greeted += 1
-
+    for o in sorted(greeted):
+        pl.semaphore_signal(barrier, inc=1, device_id=place.peer(o)[1], device_id_type=MESH)
+
+    inputs = dict(
+        params=(params_hbm, params_ref),
+        seg=(seg_hbm, seg_ref),
+        codes=(shape_code_hbm, shape_code_ref),
+        table=(table_hbm, table_ref),
+        targets=(targets_hbm, targets_ref),
+        coords=(coords_hbm, coords_ref),
+    )
+    copies = {}
+    for i, (name, (src, dst)) in enumerate(inputs.items()):
+        copies[name] = pltpu.make_async_copy(src, dst, fetched.at[i])
+        copies[name].start()
+
+    copies["params"].wait()
+    copies["seg"].wait()
     seg_heads = seg_ref[0 : head_len // LANES, :].astype(F32)
     shared = jnp.max(jnp.max(seg_heads, axis=1, keepdims=True), axis=0, keepdims=True)
-    for q in range(per_tile):
-        lanes = slice(q * LANES, (q + 1) * LANES)
-        points[0, :, lanes] = seg_ref[pl.ds(q, tiles, stride=per_tile), :].astype(F32)
-        points[1, :, lanes] = jnp.tanh(targets_ref[pl.ds(q, tiles, stride=per_tile), :] * (1.0 / CLAMP_DELTA))
-    seg = points[0]
 
     def count(where):
         return jnp.sum(jnp.sum(where.astype(F32), axis=1, keepdims=True), axis=0, keepdims=True)
 
     mine = (device * 2).astype(F32)
-    counts = [count(seg == shared), count(seg == mine), count(seg == mine + 1.0)]
+    seg_all = seg_ref[...].astype(F32)
+    counts = [count(seg_all == shared), count(seg_all == mine), count(seg_all == mine + 1.0)]
 
     phase = (device * per_device) % LANES
     own = buf.at[place.core, place.at[0], place.at[1], place.at[2]]
     raw = rows_of(params_ref, per_device)
-    raw = jnp.concatenate(
-        [raw, jnp.zeros((kept - 1 - raw.shape[0], LANES), F32), jnp.broadcast_to(counts[0], (1, LANES))], axis=0
-    )
+    while raw.shape[0] < kept - 1:
+        raw = jnp.concatenate([raw, jnp.zeros((1, LANES), F32)], axis=0)
+    raw = jnp.concatenate([raw, jnp.broadcast_to(counts[0], (1, LANES))], axis=0)
     if any(p for _, _, p, _ in bounds(2 * rows, per_device)):
         moved = pltpu.roll(raw, phase, 1)
         before = jnp.concatenate([jnp.zeros((1, LANES), F32), moved[: kept - 1]], axis=0)
         raw = jnp.where((iota((kept, LANES), 1) < phase) & (iota((kept, LANES), 0) < kept - 1), before, moved)
     own[...] = raw
+
+    pl.semaphore_wait(barrier, len(greeted) + 1)
+    gather_table, reduce_table, codes_table, spread_table = cfg["tables"]
+    gather = Gather(place, buf, gather_table, psend, precv)
+    for k in range(len(gather_table)):
+        gather.start(k, 0)
+
+    for name in ("codes", "table", "targets", "coords"):
+        copies[name].wait()
 
     base = (place.row * table_ref.shape[0]).astype(F32)
     codes_of = jnp.broadcast_to(shape_code_ref[...].astype(F32) + 1.0, (8, shapes))
@@ -534,24 +575,16 @@
     answer = dot(pick, table_ref[...], EXACT)
     codes_buf[place.core] = answer.reshape(dims + (8, CODE))
 
-    pl.semaphore_wait(barrier, greeted)
-    gather = Gather(place, buf, cfg["chunks"], cfg["gather_orders"], psend, precv)
-    chunk_ids = range(len(cfg["chunks"]))
-    for k in chunk_ids:
-        gather.start(k, 0)
-
-    codes = Reduce(place, codes_buf, codes_landing, [(0, 8)], [(2, 1, 0)], csend, crecv, False)
-    codes.start(0, 0)
-
-    for stage in range(4):
-        if stage < 3:
-            codes.arrive(0, stage)
-            if stage < 2:
-                codes.start(0, stage + 1)
-        for k in chunk_ids:
-            gather.arrive(k, stage)
-            if stage < 3:
-                gather.start(k, stage + 1)
+    codes = Reduce(place, codes_buf, codes_landing, codes_table, csend, crecv, False)
+    codes.begin()
+    for q in range(per_tile):
+        lanes = slice(q * LANES, (q + 1) * LANES)
+        points[0, :, lanes] = seg_ref[pl.ds(q, tiles, stride=per_tile), :].astype(F32)
+        points[1, :, lanes] = jnp.tanh(targets_ref[pl.ds(q, tiles, stride=per_tile), :] * (1.0 / CLAMP_DELTA))
+    seg = points[0]
+
+    for _ in itertools.zip_longest(gather.run(), codes.run()):
+        pass
     z8 = codes_buf[place.core, place.at[0], place.at[1], place.at[2]]
 
     assemble(dims, per_device, buf, flat)
@@ -565,7 +598,7 @@
     head_row = v2[H2 : H2 + 1, :]
     hbias = head_bias[:, 0:1]
 
-    total = jnp.sum(buf[:, :, :, :, kept - 8 : kept, :], axis=(0, 1, 2, 3))[7:8, 0:1]
+    total = jnp.sum(buf[:, :, :, :, kept - 1 : kept, :], axis=(0, 1, 2, 3))[:, 0:1]
     counts_all = [total]
     for k in (1, 2):
         counts_all.append(jnp.where(shared == mine + (k - 1.0), total, jnp.maximum(counts[k], 1.0)))
@@ -580,7 +613,7 @@
 
     lane1 = iota((8, 256), 1)
     sub1 = iota((8, 256), 0)
-    code1 = dot(z8, v1[0:CODE, :], EXACT) * scale1 + bias1
+    code1 = dot(z8, v1[0:CODE, :], THREE) * scale1 + bias1
     xyz1 = v1[CODE : CODE + 8, :] * scale1
     rows1 = 0.5 * jnp.where(sub1 < 3, xyz1, jnp.where(sub1 < 6, code1, 0.0))
     rows1 = jnp.where(lane1 < INNER, rows1, (lane1 == INNER + sub1).astype(F32))
@@ -590,7 +623,7 @@
     w0[...] = stack.T.astype(BF16)
 
     z_wide = turn(widen(z8, H2), INNER)
-    code2 = 0.5 * (dot(z_wide, v2[0:H2, :], EXACT) * scale2 + bias2)
+    code2 = 0.5 * (dot(z_wide, v2[0:H2, :], THREE) * scale2 + bias2)
     sub2 = iota((8, H2), 0)
     columns = jnp.where(sub2 == 6, jnp.broadcast_to(0.5 * head_row, (8, H2)), code2)
     columns = jnp.concatenate([columns, jnp.zeros((LANES - 8, H2), F32)], axis=0).T
@@ -614,7 +647,7 @@
     def lanes_of(q):
         return slice(q * LANES, (q + 1) * LANES)
 
-    def first_layer(t):
+    def first_product(t):
         at = slice(t * tile, (t + 1) * tile)
         two = points[3, t : t + 1, :]
         is_head = (t * tile + iota((1, tile), 1) < head_len).astype(F32)
@@ -623,26 +656,28 @@
         )
         xa, xb, xc = split3(x8)
         x48 = jnp.concatenate([xa, xb, xa, xb, xc, xa], axis=0).astype(BF16)
-        hc[t % 2, 768:784, :] = jnp.concatenate([xa, xb], axis=0).astype(BF16)
-        h1[...] = dot(w0[:, 0:48], x48)
+        hc[t % DEEP, 768:784, :] = jnp.concatenate([xa, xb], axis=0).astype(BF16)
+        h1[t % 2] = dot(w0[:, 0:48], x48)
+
+    def first_layer(t):
         for q in range(per_tile):
             lanes = lanes_of(q)
             for u in range(0, 256, block):
                 us = slice(u, u + block)
-                h = h1[us, lanes]
+                h = h1[t % 2, us, lanes]
                 th = jnp.tanh(h)
                 m = h * th
                 f = h + m
-                slope1[t % 2, us, lanes] = (0.5 + 0.5 * th) * (1.0 + (h - m))
+                slope1[t % DEEP, us, lanes] = (0.5 + 0.5 * th) * (1.0 + (h - m))
                 if u + block > INNER:
                     f = jnp.where(iota((block, LANES), 0) + u >= INNER, h, f)
                 fh, fl = split2(f)
-                hc[t % 2, us, lanes] = fh
-                hc[t % 2, 256 + u : 256 + u + block, lanes] = fl
-                hc[t % 2, 512 + u : 512 + u + block, lanes] = fh
+                hc[t % DEEP, us, lanes] = fh
+                hc[t % DEEP, 256 + u : 256 + u + block, lanes] = fl
+                hc[t % DEEP, 512 + u : 512 + u + block, lanes] = fh
 
     def second_product(t):
-        h2[t % 2] = dot(w2t[...], hc[t % 2, 0:768, :])
+        h2[t % 2] = dot(w2t[...], hc[t % DEEP, 0:768, :])
 
     def second_layer(t):
         parts = []
@@ -688,36 +723,30 @@
             dhead[us, :] = total_u
 
     def back_products(t):
-        df[...] = dot(w2b[...], d2b[t % 2])
-        dw2[...] = dw2[...] + dot_nt(hc[t % 2, 512:784, :], d2b[t % 2])
+        df[t % 2] = dot(w2b[...], d2b[t % 2])
+        dw2[...] = dw2[...] + dot_nt(hc[t % DEEP, 512:784, :], d2b[t % 2])
 
     def back_first(t):
         for u in range(0, 256, block):
             us = slice(u, u + block)
-            d1b[us, :] = (df[us, :] * slope1[t % 2, us, :]).astype(BF16)
-        dw1[...] = dw1[...] + dot_nt(hc[t % 2, 768:784, :], d1b[...])
-
-    first_layer(0)
-    for t in range(tiles + 1):
-        if t < tiles:
-            second_product(t)
-        if t > 0:
-            back_second(t - 1)
-            back_products(t - 1)
-        if t < tiles:
-            second_layer(t)
-        if t > 0:
-            back_first(t - 1)
-        if t + 1 < tiles:
-            first_layer(t + 1)
+            d1b[t % 2, us, :] = (df[t % 2, us, :] * slope1[t % DEEP, us, :]).astype(BF16)
+
+    def back_first_product(t):
+        dw1[...] = dw1[...] + dot_nt(hc[t % DEEP, 768:784, :], d1b[t % 2])
+
+    steps = ((first_product, 2), (second_product, 0), (first_layer, 1), (second_layer, -1), (back_products, -3), (back_second, -2), (back_first_product, -5), (back_first, -4))
+    for i in range(-max(lag for _, lag in steps), tiles - min(lag for _, lag in steps)):
+        for stage, lag in steps:
+            if 0 <= i + lag < tiles:
+                stage(i + lag)
 
     outer1 = jnp.where(lane1 < INNER, dw1[0:8, :] + dw1[8:16, :], 0.0)
     outer2 = dw2[256:264, :] + dw2[264:272, :]
     slot_rows = (sub1 >= 3) & (sub1 < 6)
     d1 = jnp.where(slot_rows, outer1, 0.0)
     d2 = jnp.where((sub2 >= 3) & (sub2 < 6), outer2, 0.0)
-    dz = dot_nt(d1 * scale1, v1[0:CODE, :], EXACT)
-    dz = dz + turn(dot_nt(d2 * scale2, v2[0:H2, :], EXACT), -INNER)[:, 0:CODE]
+    dz = dot_nt(d1 * scale1, v1[0:CODE, :], THREE)
+    dz = dz + turn(dot_nt(d2 * scale2, v2[0:H2, :], THREE), -INNER)[:, 0:CODE]
     own_rows = (sub1 == 4) | (sub1 == 5)
     dz = dz + jnp.where(own_rows, (2.0 * PRIOR_WEIGHT / shapes) * z8, 0.0)
     prior = jnp.where(own_rows, z8 * z8, 0.0)
@@ -726,19 +755,21 @@
     message = jnp.where(slot_rows, dz, 0.0)
     message = jnp.where(sub1 == 0, jnp.broadcast_to(loss_here, (8, CODE)), message)
     grads_buf[place.core, place.at[0], place.at[1], place.at[2]] = message
-    spread = Gather(place, grads_buf, [(0, 8)], [(0, 1, 2)], dsend, drecv)
+    spread = Gather(place, grads_buf, spread_table, dsend, drecv)
     spread.start(0, 0)
 
-    g1[0:CODE, :] = dot_tn(z8, d1, EXACT)
+    g1[0:CODE, :] = dot_tn(z8, d1, THREE)
     g1[CODE : CODE + 8, :] = jnp.where(sub1 < 3, outer1, 0.0)
     along1 = jnp.sum(v1[...] * g1[...], axis=0, keepdims=True)
     g1[...] = g1[...] * scale1 - v1[...] * (scale1 * inv1 * inv1 * along1)
-    g2[0:H2, :] = dot_tn(z_wide, d2, EXACT)
+    g2[0:H2, :] = dot_tn(z_wide, d2, THREE)
     g2[0:256, :] = g2[0:256, :] + jnp.where(iota((256, H2), 0) < INNER, dw2[0:256, :], 0.0)
     g2[H2 - 8 : H2, :] = g2[H2 - 8 : H2, :] + jnp.where(sub2 >= 5, dw2[248:256, :], 0.0)
     along2 = jnp.sum(v2[0:H2, :] * g2[0:H2, :], axis=0, keepdims=True)
     g2[0:H2, :] = g2[0:H2, :] * scale2 - v2[0:H2, :] * (scale2 * inv2 * inv2 * along2)
-    g2[H2 : H2 + 8, :] = dot_nt(jnp.ones((8, LANES), F32), dhead[...], EXACT)
+    high, low = split2(dhead[...])
+    ones = jnp.ones((16, LANES), BF16)
+    g2[H2 : H2 + 8, :] = (dot_nt(ones, high) + dot_nt(ones, low))[0:8, :]
     dbias = jnp.broadcast_to(jnp.sum(sums[1:2, :], axis=1, keepdims=True), (1, LANES))
     pack_first(g1, wide, flat)
     pack_second(g2, flat)
@@ -755,23 +786,13 @@
     gather.finish()
     codes.finish()
     scatter(dims, per_device, kept, flat, buf)
-    reduce = Reduce(place, buf, landing, cfg["chunks"], cfg["reduce_orders"], rsend, rrecv, True)
-    for k in chunk_ids:
-        reduce.start(k, -1)
-    for stage in range(-1, 3):
-        for k in chunk_ids:
-            reduce.arrive(k, stage)
-            if stage < 2:
-                reduce.start(k, stage + 1)
-        spread.arrive(0, stage + 1)
-        if stage < 2:
-            spread.start(0, stage + 2)
-    piece = own[...]
-    if any(p for _, _, p, _ in bounds(2 * rows, per_device)):
-        moved = pltpu.roll(piece, (LANES - phase) % LANES, 1)
-        after = jnp.concatenate([moved[1:], moved[:1]], axis=0)
-        piece = jnp.where(iota((kept, LANES), 1) < LANES - phase, moved, after)
-    grad_ref[...] = piece
+    reduce = Reduce(place, buf, landing, reduce_table, rsend, rrecv, True)
+    reduce.begin()
+    arriving, summing = spread.run(), reduce.run()
+    for _ in range(2):
+        next(summing)
+        next(arriving)
+    next(arriving)
 
     everyone = grads_buf[...].reshape(2 * slots, CODE)
     kind = iota((shapes, 2 * slots), 1) & 7
@@ -785,24 +806,31 @@
     code_rows = table_ref.shape[0]
     target_row = dot(codes_of, asked, EXACT)[0:1, :] - 1.0 - base
     pick = (target_row == iota((code_rows, 2 * slots), 0).astype(F32)).astype(F32)
-    grad_table = dot(pick, everyone, EXACT)
-    here_codes = (codes_of[0:1, :] - 1.0 - base) == iota((code_rows, shapes), 0).astype(F32)
-    is_used = jnp.sum(here_codes.astype(F32), axis=1, keepdims=True) > 0.5
+    grad_table = dot(pick, everyone, THREE)
     grad_table_ref[...] = grad_table
-    used_ref[...] = jnp.broadcast_to(is_used.astype(F32), used_ref.shape)
     loss_ref[...] = jnp.sum(grads_buf[:, :, :, :, 0:8, 0:LANES], axis=(0, 1, 2, 3))[0:1, 0:1]
+    next(summing)
+    piece = own[...]
+    if any(p for _, _, p, _ in bounds(2 * rows, per_device)):
+        moved = pltpu.roll(piece, (LANES - phase) % LANES, 1)
+        after = jnp.concatenate([moved[1:], moved[:1]], axis=0)
+        piece = jnp.where(iota((kept, LANES), 1) < LANES - phase, moved, after)
+    grad_ref[...] = piece
+
     spread.finish()
     reduce.finish()
 
 
-def chunked(rows, count):
-    blocks = rows // 8
-    count = min(count, blocks)
-    out, at = [], 0
-    for k in range(count):
-        size = (blocks * (k + 1)) // count * 8 - at
-        out.append((at, size))
-        at += size
+def chunked(rows, parts):
+    blocks = -(-rows // 8)
+    whole = sum(share for share, _ in parts)
+    out, at, upto = [], 0, 0
+    for share, order in parts:
+        upto += share
+        end = min((blocks * upto + whole // 2) // whole * 8, rows)
+        if end > at:
+            out.append((at, end - at, order))
+        at = end
     return out
 
 
@@ -812,29 +840,37 @@
     used, kept = piece_rows(per_device, devices)
     dims = chip_dims(rows)
     points_here = segment_ids.shape[0]
-    tile = 1024
+    tile = 256
     tiles = points_here // tile
     shapes = shape_code.shape[0]
     code_rows = table.shape[0]
-    chunks = chunked(kept, 4)
+    out_first, out_last = ((0,), (1, 2)), ((1, 2), (0,))
+    tables = [
+        chunked(kept, [(4, out_first), (4, out_first), (3, out_last)]),
+        chunked(kept, [(4, out_last), (4, out_last), (3, out_first)]),
+        [(0, 8, out_last)],
+        [(0, 8, out_first)],
+    ]
     cfg = dict(
         dims=dims,
         rows=rows,
         per_device=per_device,
         tile=tile,
         shapes=shapes,
-        chunks=chunks,
-        gather_orders=[(0, 1, 2), (0, 2, 1)],
-        reduce_orders=[(1, 2, 0), (2, 1, 0)],
+        tables=tables,
     )
     flat_rows = per_device * devices // LANES + kept + 8
-    most = max(dims)
-    n = len(chunks)
     vm = pltpu.VMEM
-    dma = pltpu.SemaphoreType.DMA
     scratch = [
+        vm((per_device,), F32),
+        vm((code_rows, CODE), F32),
+        vm((3, points_here), F32),
+        vm((points_here // LANES, LANES), F32),
+        vm((points_here // LANES, LANES), jnp.int32),
+        vm((1, shapes), jnp.int32),
+        pltpu.SemaphoreType.DMA((6,)),
         vm((2,) + dims + (kept, LANES), F32),
-        landings(dims, cfg["reduce_orders"], (kept, LANES)),
+        landings(dims, tables[1], LANES, True),
         vm((flat_rows, LANES), F32),
         vm((272, 256), F32),
         vm((264, 256), F32),
@@ -847,43 +883,38 @@
         vm((3, H2, LANES), F32),
         vm((H2, LANES), F32),
         vm((4, tiles, tile), F32),
-        vm((2, 784, tile), BF16),
-        vm((256, tile), F32),
+        vm((DEEP, 784, tile), BF16),
         vm((2, 256, tile), F32),
+        vm((DEEP, 256, tile), F32),
         vm((2, H2, tile), F32),
         vm((2, H2, tile), F32),
         vm((2, H2, tile), F32),
         vm((2, 8, tile), F32),
         vm((2, H2, tile), BF16),
-        vm((256, tile), F32),
-        vm((256, tile), BF16),
+        vm((2, 256, tile), F32),
+        vm((2, 256, tile), BF16),
         vm((272, H2), F32),
         vm((16, 256), F32),
         vm((H2, LANES), F32),
         vm((8, tile), F32),
         vm((2,) + dims + (8, CODE), F32),
-        landings(dims, [(2, 1, 0)], (8, CODE)),
+        landings(dims, tables[2], CODE, False),
         vm((2,) + dims + (8, CODE), F32),
-        dma((n, 4, most)),
-        dma((n, 4, most)),
-        dma((1, 4, most)),
-        dma((1, 4, most)),
-        dma((1, 4, most)),
-        dma((1, 4, most)),
-        dma((n, 4, most)),
-        dma((n, 4, most)),
+        *semaphores(dims, tables[0]),
+        *semaphores(dims, tables[2]),
+        *semaphores(dims, tables[3]),
+        *semaphores(dims, tables[1]),
     ]
     spec = pl.BlockSpec(memory_space=pltpu.VMEM)
-    loss, grad, grad_table, marks = pl.pallas_call(
+    loss, grad, grad_table = pl.pallas_call(
         functools.partial(kernel, cfg),
         out_shape=(
             jax.ShapeDtypeStruct((1, 1), F32),
             jax.ShapeDtypeStruct((kept, LANES), F32),
             jax.ShapeDtypeStruct((code_rows, CODE), F32),
-            jax.ShapeDtypeStruct((code_rows, CODE), F32),
         ),
-        in_specs=[spec] * 6,
-        out_specs=(spec,) * 4,
+        in_specs=[pl.BlockSpec(memory_space=pl.ANY)] * 6,
+        out_specs=(spec,) * 3,
         scratch_shapes=scratch,
         compiler_params=pltpu.CompilerParams(
             collective_id=0, has_side_effects=True, vmem_limit_bytes=56 << 20
@@ -903,7 +934,7 @@
         out_shape=(jax.ShapeDtypeStruct((1, 1), F32),) + (flat_out,) * 3 + (table_out,) * 3,
         in_specs=[spec] * 10,
         out_specs=(spec,) * 7,
-    )(grad, grad_table, marks, loss, params, momentum, average, table, code_first, code_second)
+    )(grad, grad_table, shape_code.reshape(1, shapes), loss, params, momentum, average, table, code_first, code_second)
     return (outs[0].reshape(()),) + tuple(outs[1:])
 
 

time: 57.3 us -> 49.3 us (0.86)
  Pallas kernels: 56.5 us -> 48.4 us
    pallas_call x1, Pallas kernels: 54 us -> 45.9 us  [shards(): pl.pallas_call(functools.partial(kernel, cfg), out_shape=(jax.ShapeDtypeS...]
where the time goes in v3:
time: 49.3 us; the launch traced here: 49.1 us
  Pallas kernels  48.4 us (98%)
  between operations  0.64 us (1%)
    pallas_call x1, Pallas kernels, shards(): pl.pallas_call(functools.partial(kernel, cfg), out_shape=(jax.ShapeDtypeS...  45.9 us
    pallas_call x1, Pallas kernels, shards(): pl.pallas_call(functools.partial(update, per_device), out_shape=(jax.Shap...  2.5 us

profile of v3, /device:TPU:0, one launch (start us, length us, event | category | flops | bytes accessed | tf_op | source)
XLA Modules:
  0.0 49.1 jit_solution(13993530311107500451)
XLA Ops:
  0.6 45.9 %shard_map.153 = (f32[1,1]{1,0:T(1,128)}, f32[82,128]{1,0:T(8,128)}, f32[64,256]{1,0:T(8,128)}) custom-call(f32[10304]{0:T(1024)} %params_ref.1, f32[64,256]{1,0:T(8,128)} %table_ref.1, f32[3,4096]{1,0:T(4,128)} %coords_hbm.1, f32[32,128]{1,0:T(8,128)} %bitcast.4, s32[32,128]{1,0:T(8,128)} %bitcast.5, s32[1,64]{1,0:T(1,128)} %bitcast.6), custom_call_target="tpu_custom_call" | custom-call | tf_op jit(solution)/shard_map/pallas_call | solution.py:909
  46.6 2.5 %shard_map.154 = (f32[1,1]{1,0:T(1,128)}, f32[10304]{0:T(1024)}, f32[10304]{0:T(1024)}, f32[10304]{0:T(1024)}, f32[64,256]{1,0:T(8,128)}, /*index=5*/f32[64,256]{1,0:T(8,128)}, f32[64,256]{1,0:T(8,128)}) custom-call(f32[82,128]{1,0:T(8,128)} %get-tuple-element.17.grad_ref, f32[64,256]{1,0:T(8,128)} %get-tuple-element.18.grad_table_ref, s32[1,64]{1,0:T(1,128)} %bitcast.7, ...), custom_call_target="tpu_custom_call" | custom-call | tf_op jit(solution)/shard_map/pallas_call | solution.py:932

commit v4 on v3

--- a/solution.py
+++ b/solution.py
@@ -632,7 +632,7 @@
     head[...] = jnp.broadcast_to(columns[:, 6:7], (H2, LANES))
     last = jnp.where(sub2 < 5, v2[248:256, :], v2[H2 - 8 : H2, :])
     normal = jnp.concatenate([v2[0:248, :], last], axis=0) * scale2
-    w2b[...] = normal.astype(BF16)
+    w2b[...] = (normal * (0.25 * head_row)).astype(BF16)
     high, low = split2(0.5 * normal.T)
     w2t[:, 0:256] = high
     w2t[:, 256:512] = high
@@ -658,6 +658,7 @@
         x48 = jnp.concatenate([xa, xb, xa, xb, xc, xa], axis=0).astype(BF16)
         hc[t % DEEP, 768:784, :] = jnp.concatenate([xa, xb], axis=0).astype(BF16)
         h1[t % 2] = dot(w0[:, 0:48], x48)
+        yield
 
     def first_layer(t):
         for q in range(per_tile):
@@ -668,16 +669,19 @@
                 th = jnp.tanh(h)
                 m = h * th
                 f = h + m
-                slope1[t % DEEP, us, lanes] = (0.5 + 0.5 * th) * (1.0 + (h - m))
+                slope1[t % DEEP, us, lanes] = (1.0 + th) * (1.0 + (h - m))
                 if u + block > INNER:
                     f = jnp.where(iota((block, LANES), 0) + u >= INNER, h, f)
                 fh, fl = split2(f)
                 hc[t % DEEP, us, lanes] = fh
                 hc[t % DEEP, 256 + u : 256 + u + block, lanes] = fl
                 hc[t % DEEP, 512 + u : 512 + u + block, lanes] = fh
+                yield
 
     def second_product(t):
-        h2[t % 2] = dot(w2t[...], hc[t % DEEP, 0:768, :])
+        for m in range(0, H2, 256):
+            h2[t % 2, m : m + 256, :] = dot(w2t[m : m + 256, :], hc[t % DEEP, 0:768, :])
+            yield
 
     def second_layer(t):
         parts = []
@@ -695,10 +699,11 @@
                 s = h + m
                 hw = head[us, :]
                 second[t % 2, us, lanes] = s
-                act[t % 2, us, lanes] = hw * ((1.0 + th) * (1.0 + (h - m)))
+                act[t % 2, us, lanes] = (1.0 + th) * (1.0 + (h - m))
                 w = hw * s
                 for v in range(0, block, 8):
                     part = part + w[v : v + 8]
+                yield
             parts.append(jnp.sum(part, axis=0, keepdims=True))
         preds[t % 2, 0:1, :] = 2.0 * jnp.concatenate(parts, axis=1) + hbias
 
@@ -721,26 +726,41 @@
                 d2b[t % 2, us, lanes] = (act[t % 2, us, lanes] * dp).astype(BF16)
                 total_u = total_u + second[t % 2, us, lanes] * dp
             dhead[us, :] = total_u
+            yield
 
     def back_products(t):
         df[t % 2] = dot(w2b[...], d2b[t % 2])
-        dw2[...] = dw2[...] + dot_nt(hc[t % DEEP, 512:784, :], d2b[t % 2])
+        yield
+        for n in range(0, H2, 256):
+            dw2[:, n : n + 256] = dw2[:, n : n + 256] + dot_nt(hc[t % DEEP, 512:784, :], d2b[t % 2, n : n + 256, :])
+            yield
 
     def back_first(t):
         for u in range(0, 256, block):
             us = slice(u, u + block)
             d1b[t % 2, us, :] = (df[t % 2, us, :] * slope1[t % DEEP, us, :]).astype(BF16)
+            yield
 
     def back_first_product(t):
         dw1[...] = dw1[...] + dot_nt(hc[t % DEEP, 768:784, :], d1b[t % 2])
-
-    steps = ((first_product, 2), (second_product, 0), (first_layer, 1), (second_layer, -1), (back_products, -3), (back_second, -2), (back_first_product, -5), (back_first, -4))
-    for i in range(-max(lag for _, lag in steps), tiles - min(lag for _, lag in steps)):
-        for stage, lag in steps:
-            if 0 <= i + lag < tiles:
-                stage(i + lag)
+        yield
+
+    products = ((second_product, 0), (back_products, -3), (first_product, 2), (back_first_product, -5))
+    elementwise = ((back_second, -2), (second_layer, -1), (first_layer, 1), (back_first, -4))
+    for i in range(-2, tiles + 5):
+
+        def pieces(stages):
+            return itertools.chain(*(stage(i + lag) for stage, lag in stages if 0 <= i + lag < tiles))
+
+        rest = pieces(elementwise)
+        for _ in pieces(products):
+            for _ in itertools.islice(rest, 8):
+                pass
+        for _ in rest:
+            pass
 
     outer1 = jnp.where(lane1 < INNER, dw1[0:8, :] + dw1[8:16, :], 0.0)
+    dw2[...] = dw2[...] * (0.5 * head_row)
     outer2 = dw2[256:264, :] + dw2[264:272, :]
     slot_rows = (sub1 >= 3) & (sub1 < 6)
     d1 = jnp.where(slot_rows, outer1, 0.0)

time: 49.3 us -> 48.5 us (0.984)
  Pallas kernels: 48.4 us -> 47.6 us
    pallas_call x1, Pallas kernels: 45.9 us -> 45.1 us  [shards(): pl.pallas_call(functools.partial(kernel, cfg), out_shape=(jax.ShapeDtypeS...]
where the time goes in v4:
time: 48.5 us; the launch traced here: 48.3 us
  Pallas kernels  47.6 us (98%)
  between operations  0.64 us (1%)
    pallas_call x1, Pallas kernels, shards(): pl.pallas_call(functools.partial(kernel, cfg), out_shape=(jax.ShapeDtypeS...  45.1 us
    pallas_call x1, Pallas kernels, shards(): pl.pallas_call(functools.partial(update, per_device), out_shape=(jax.Shap...  2.5 us

profile of v4, /device:TPU:0, one launch (start us, length us, event | category | flops | bytes accessed | tf_op | source)
XLA Modules:
  0.0 48.3 jit_solution(3029832370590259295)
XLA Ops:
  0.6 45.1 %shard_map.153 = (f32[1,1]{1,0:T(1,128)}, f32[82,128]{1,0:T(8,128)}, f32[64,256]{1,0:T(8,128)}) custom-call(f32[10304]{0:T(1024)} %params_ref.1, f32[64,256]{1,0:T(8,128)} %table_ref.1, f32[3,4096]{1,0:T(4,128)} %coords_hbm.1, f32[32,128]{1,0:T(8,128)} %bitcast.4, s32[32,128]{1,0:T(8,128)} %bitcast.5, s32[1,64]{1,0:T(1,128)} %bitcast.6), custom_call_target="tpu_custom_call" | custom-call | tf_op jit(solution)/shard_map/pallas_call | solution.py:929
  45.8 2.5 %shard_map.154 = (f32[1,1]{1,0:T(1,128)}, f32[10304]{0:T(1024)}, f32[10304]{0:T(1024)}, f32[10304]{0:T(1024)}, f32[64,256]{1,0:T(8,128)}, /*index=5*/f32[64,256]{1,0:T(8,128)}, f32[64,256]{1,0:T(8,128)}) custom-call(f32[82,128]{1,0:T(8,128)} %get-tuple-element.17.grad_ref, f32[64,256]{1,0:T(8,128)} %get-tuple-element.18.grad_table_ref, s32[1,64]{1,0:T(1,128)} %bitcast.7, ...), custom_call_target="tpu_custom_call" | custom-call | tf_op jit(solution)/shard_map/pallas_call | solution.py:952

commit v5 on v4

--- a/solution.py
+++ b/solution.py
@@ -317,12 +317,13 @@
             flat[row : row + count, :] = src[0:count, :]
 
 
-def scatter(dims, per_device, rows_kept, flat, buf):
+def scatter(dims, per_device, chunk, flat, buf):
     rows = dims[0] * dims[1] * dims[2]
     for d, row, phase, count in bounds(2 * rows, per_device):
         chip = d // 2
         dst = buf.at[d % 2, chip // (dims[1] * dims[2]), (chip // dims[2]) % dims[1], chip % dims[2]]
-        dst[...] = flat[row : row + rows_kept, :]
+        begin, size, _ = chunk
+        dst[begin : begin + size, :] = flat[row + begin : row + begin + size, :]
 
 
 def first_blocks():
@@ -527,34 +528,35 @@
         copies[name].start()
 
     copies["params"].wait()
-    copies["seg"].wait()
-    seg_heads = seg_ref[0 : head_len // LANES, :].astype(F32)
-    shared = jnp.max(jnp.max(seg_heads, axis=1, keepdims=True), axis=0, keepdims=True)
-
-    def count(where):
-        return jnp.sum(jnp.sum(where.astype(F32), axis=1, keepdims=True), axis=0, keepdims=True)
-
-    mine = (device * 2).astype(F32)
-    seg_all = seg_ref[...].astype(F32)
-    counts = [count(seg_all == shared), count(seg_all == mine), count(seg_all == mine + 1.0)]
-
     phase = (device * per_device) % LANES
     own = buf.at[place.core, place.at[0], place.at[1], place.at[2]]
     raw = rows_of(params_ref, per_device)
     while raw.shape[0] < kept - 1:
         raw = jnp.concatenate([raw, jnp.zeros((1, LANES), F32)], axis=0)
-    raw = jnp.concatenate([raw, jnp.broadcast_to(counts[0], (1, LANES))], axis=0)
     if any(p for _, _, p, _ in bounds(2 * rows, per_device)):
         moved = pltpu.roll(raw, phase, 1)
-        before = jnp.concatenate([jnp.zeros((1, LANES), F32), moved[: kept - 1]], axis=0)
-        raw = jnp.where((iota((kept, LANES), 1) < phase) & (iota((kept, LANES), 0) < kept - 1), before, moved)
-    own[...] = raw
+        before = jnp.concatenate([jnp.zeros((1, LANES), F32), moved[: kept - 2]], axis=0)
+        raw = jnp.where(iota((kept - 1, LANES), 1) < phase, before, moved)
+    own[0 : kept - 1, :] = raw
 
     pl.semaphore_wait(barrier, len(greeted) + 1)
     gather_table, reduce_table, codes_table, spread_table = cfg["tables"]
     gather = Gather(place, buf, gather_table, psend, precv)
-    for k in range(len(gather_table)):
+    for k in range(len(gather_table) - 1):
         gather.start(k, 0)
+
+    copies["seg"].wait()
+    seg_heads = seg_ref[0 : head_len // LANES, :].astype(F32)
+    shared = jnp.max(jnp.max(seg_heads, axis=1, keepdims=True), axis=0, keepdims=True)
+
+    def count(where):
+        return jnp.sum(jnp.sum(where.astype(F32), axis=1, keepdims=True), axis=0, keepdims=True)
+
+    mine = (device * 2).astype(F32)
+    seg_all = seg_ref[...].astype(F32)
+    counts = [count(seg_all == shared), count(seg_all == mine), count(seg_all == mine + 1.0)]
+    own[kept - 1 : kept, :] = jnp.broadcast_to(counts[0], (1, LANES))
+    gather.start(len(gather_table) - 1, 0)
 
     for name in ("codes", "table", "targets", "coords"):
         copies[name].wait()
@@ -805,9 +807,10 @@
     )
     gather.finish()
     codes.finish()
-    scatter(dims, per_device, kept, flat, buf)
     reduce = Reduce(place, buf, landing, reduce_table, rsend, rrecv, True)
-    reduce.begin()
+    for k, chunk in enumerate(reduce_table):
+        scatter(dims, per_device, chunk, flat, buf)
+        reduce.start(k, -1)
     arriving, summing = spread.run(), reduce.run()
     for _ in range(2):
         next(summing)
@@ -866,8 +869,8 @@
     code_rows = table.shape[0]
     out_first, out_last = ((0,), (1, 2)), ((1, 2), (0,))
     tables = [
-        chunked(kept, [(4, out_first), (4, out_first), (3, out_last)]),
-        chunked(kept, [(4, out_last), (4, out_last), (3, out_first)]),
+        chunked(kept, [(4, out_first), (3, out_first), (4, out_last)]),
+        chunked(kept, [(3, out_first), (4, out_last), (4, out_last)]),
         [(0, 8, out_last)],
         [(0, 8, out_first)],
     ]

time: 48.5 us -> 48.2 us (level)
  no operation moved by 1% of the time
where the time goes in v5:
time: 48.2 us; the launch traced here: 47.9 us
  Pallas kernels  47.3 us (98%)
  between operations  0.64 us (1%)
    pallas_call x1, Pallas kernels, shards(): pl.pallas_call(functools.partial(kernel, cfg), out_shape=(jax.ShapeDtypeS...  44.8 us
    pallas_call x1, Pallas kernels, shards(): pl.pallas_call(functools.partial(update, per_device), out_shape=(jax.Shap...  2.5 us

profile of v5, /device:TPU:0, one launch (start us, length us, event | category | flops | bytes accessed | tf_op | source)
XLA Modules:
  0.0 47.9 jit_solution(15037919808062086892)
XLA Ops:
  0.6 44.8 %shard_map.153 = (f32[1,1]{1,0:T(1,128)}, f32[82,128]{1,0:T(8,128)}, f32[64,256]{1,0:T(8,128)}) custom-call(f32[10304]{0:T(1024)} %params_ref.1, f32[64,256]{1,0:T(8,128)} %table_ref.1, f32[3,4096]{1,0:T(4,128)} %coords_hbm.1, f32[32,128]{1,0:T(8,128)} %bitcast.4, s32[32,128]{1,0:T(8,128)} %bitcast.5, s32[1,64]{1,0:T(1,128)} %bitcast.6), custom_call_target="tpu_custom_call" | custom-call | tf_op jit(solution)/shard_map/pallas_call | solution.py:932
  45.4 2.5 %shard_map.154 = (f32[1,1]{1,0:T(1,128)}, f32[10304]{0:T(1024)}, f32[10304]{0:T(1024)}, f32[10304]{0:T(1024)}, f32[64,256]{1,0:T(8,128)}, /*index=5*/f32[64,256]{1,0:T(8,128)}, f32[64,256]{1,0:T(8,128)}) custom-call(f32[82,128]{1,0:T(8,128)} %get-tuple-element.17.grad_ref, f32[64,256]{1,0:T(8,128)} %get-tuple-element.18.grad_table_ref, s32[1,64]{1,0:T(1,128)} %bitcast.7, ...), custom_call_target="tpu_custom_call" | custom-call | tf_op jit(solution)/shard_map/pallas_call | solution.py:955
